TPU v7x, 512 devices: a whole 4x8x8 slice. The times are simulated.
512 devices in a mesh: gx: 16 (over y, core), gy: 32 (over z, x).
Axes of the slice: x: 4, y: 8, z: 8, core: 2. Of those that a mesh axis runs over, the one named last changes fastest.
Arguments:
- right_side: float32 [688, 928, 128], P('gx', 'gy'), may hold values from -6 to 6
- diffusion: float32 [96, 128, 18], P('gx', 'gy'), may hold values from 0.2 to 5
- inverse_correlation_squared: float32 [96, 128, 18], P('gx', 'gy'), may hold values from 0.5 to 8
- widths_x: int32 [16], P('gx'), may hold values from 1 to 6, 48 in all
- widths_y: int32 [32], P('gy'), may hold values from 1 to 4, 64 in all
- coarse_factor: float32 [8192, 8192], P(('gx', 'gy')), may hold values from -0.00390625 to 0.00390625
Outputs:
- solution_field: float32 [688, 928, 128], P('gx', 'gy')
- residual: float32 [688, 928, 128], P('gx', 'gy')
Inputs may be any that keep to these rules, and one draw needn't show every extreme that they name: `widths_x`: each entry is the element columns of one partition along the first direction; they sum to 3 times the number of partitions along gx, and some partition has exactly 6. `widths_y`: each entry is the element columns of one partition along the second direction; they sum to 2 times the number of partitions along gy, and some partition has exactly 4.
All inputs are finite; a program needn't handle non-finite values. No bound on the sum of `widths_x` or of `widths_y` on one device may be relied on, other than what follows from the above.
Results may differ from a plain program's by a relative error of at most 0.029.
Values sent between devices are 32-bit elements; how exact they have to be, the bound alone decides.
A program may use at most 64 MiB of HBM per device.

v0:
```python
import jax
import jax.numpy as jnp
import numpy as np
from jax import lax
from jax.sharding import PartitionSpec as P

ITERS = 3


HIGHEST = lax.Precision.HIGHEST


def padded(cells, sides, width):
    for axis, dim in sides:
        count = lax.axis_size(axis)
        ends = count - 1
        head = lax.slice_in_dim(cells, 0, width, axis=dim)
        tail = lax.slice_in_dim(cells, cells.shape[dim] - width, cells.shape[dim], axis=dim)
        cells = jnp.concatenate(
            [
                lax.ppermute(tail, axis, [(i, (i + 1) % count) for i in range(ends)]),
                cells,
                lax.ppermute(head, axis, [((i + 1) % count, i) for i in range(ends)]),
            ],
            axis=dim,
        )
    return cells


def gll_weights():
    return np.array(
        [
            1.0 / 28.0,
            0.2107042271435061,
            0.3411226924835044,
            0.4124587946587038,
            0.4124587946587038,
            0.3411226924835044,
            0.2107042271435061,
            1.0 / 28.0,
        ]
    )


def gll_derivative():
    points = np.array(
        [
            -1.0,
            -0.8717401485096066,
            -0.5917001814331423,
            -0.2092992179024789,
            0.2092992179024789,
            0.5917001814331423,
            0.8717401485096066,
            1.0,
        ]
    )
    identity = np.eye(8) > 0
    spacing = np.where(identity, 1.0, points[:, None] - points[None, :])
    barycentric = 1.0 / np.prod(spacing, axis=1)
    matrix = np.where(identity, 0.0, barycentric[None, :] / barycentric[:, None] / spacing)
    return np.where(identity, -np.sum(matrix, axis=1)[:, None], matrix)


def storage_nodes(width, capacity):
    slots = jnp.arange(7 * capacity + 1, dtype=jnp.int32)
    return jnp.where(slots < 7 * width, slots, jnp.where(slots == 7 * capacity, 7 * width, -1))


def axis_tables(nodes, width, capacity):
    weights = gll_weights()
    derivative = gll_derivative()
    points = np.arange(8 * capacity)
    element = jnp.asarray(points // 8, jnp.int32)
    offset = nodes[None, :] - 7 * element[:, None]
    usable = (nodes[None, :] >= 0) & (offset >= 0) & (offset <= 7) & (element[:, None] < width)
    matches = offset[:, :, None] == jnp.arange(8, dtype=jnp.int32)[None, None, :]
    rows = jnp.asarray(derivative[points % 8], jnp.float32)
    table = jnp.where(usable, jnp.sum(jnp.where(matches, rows[:, None, :], 0.0), axis=2), 0.0)
    owners = jnp.arange(capacity, dtype=jnp.int32)
    owner_offset = nodes[None, :] - 7 * owners[:, None]
    owner_usable = (
        (nodes[None, :] >= 0)
        & (owner_offset >= 0)
        & (owner_offset <= 7)
        & (owners[:, None] < width)
    )
    owner_matches = owner_offset[:, :, None] == jnp.arange(8, dtype=jnp.int32)[None, None, :]
    weight_row = jnp.asarray(weights, jnp.float32)
    weight_table = jnp.where(
        owner_usable, jnp.sum(jnp.where(owner_matches, weight_row[None, None, :], 0.0), axis=2), 0.0
    )
    point_weights = jnp.where(element < width, jnp.asarray(weights[points % 8], jnp.float32), 0.0)
    return (table, weight_table, point_weights)


def axis_share(nodes, position, count):
    slots = jnp.arange(nodes.shape[0], dtype=jnp.int32)
    halved = (slots == 0) & (position > 0) | (slots == nodes.shape[0] - 1) & (position < count - 1)
    return jnp.where(nodes >= 0, jnp.where(halved, 0.5, 1.0), 0.0).astype(jnp.float32)


def assemble(values):
    neighbours = padded(values, (("gx", 0),), 1)
    result = values.at[0].add(neighbours[0]).at[-1].add(neighbours[-1])
    beside = padded(result, (("gy", 1),), 1)
    result = result.at[:, 0].add(beside[:, 0]).at[:, -1].add(beside[:, -1])
    return result


def inner(first, second, weight_cells):
    return lax.psum(jnp.sum(weight_cells * first * second), ("gx", "gy"))


def body(right_side, diffusion, inverse_correlation_squared, widths_x, widths_y, coarse_factor):
    row_count = lax.axis_size("gx")
    column_count = lax.axis_size("gy")
    row_place = lax.axis_index("gx")
    column_place = lax.axis_index("gy")
    capacity_first, capacity_second, layers = diffusion.shape
    depth = right_side.shape[2]
    nodes_first = storage_nodes(widths_x[0], capacity_first)
    nodes_second = storage_nodes(widths_y[0], capacity_second)
    depth_slots = jnp.arange(depth, dtype=jnp.int32)
    vertical_node_count = jnp.where(depth_slots <= 7 * layers, depth_slots, -1)
    table_first, weight_first, points_first = axis_tables(nodes_first, widths_x[0], capacity_first)
    table_second, weight_second, points_second = axis_tables(
        nodes_second, widths_y[0], capacity_second
    )
    table_vertical, weight_vertical, points_vertical = axis_tables(
        vertical_node_count, layers, layers
    )
    plane_second = jnp.einsum(
        "efh,fy,hk->eyk", diffusion, weight_second, weight_vertical, precision=HIGHEST
    )
    coef_first = jnp.repeat(plane_second, 8, axis=0) * points_first[:, None, None]
    plane_first = jnp.einsum(
        "efh,ex,hk->xfk", diffusion, weight_first, weight_vertical, precision=HIGHEST
    )
    coef_second = jnp.repeat(plane_first, 8, axis=1) * points_second[None, :, None]
    plane_both = jnp.einsum(
        "efh,ex,fy->xyh", diffusion, weight_first, weight_second, precision=HIGHEST
    )
    coef_vertical = jnp.repeat(plane_both, 8, axis=2) * points_vertical[None, None, :]
    mass = jnp.einsum(
        "efh,ex,fy,hk->xyk",
        inverse_correlation_squared,
        weight_first,
        weight_second,
        weight_vertical,
        precision=HIGHEST,
    )
    diagonal_local = (
        mass
        + jnp.einsum("qs,qyk->syk", table_first * table_first, coef_first, precision=HIGHEST)
        + jnp.einsum("qs,xqk->xsk", table_second * table_second, coef_second, precision=HIGHEST)
        + jnp.einsum(
            "xyq,qk->xyk", coef_vertical, table_vertical * table_vertical, precision=HIGHEST
        )
    )
    share_first = axis_share(nodes_first, row_place, row_count)
    share_second = axis_share(nodes_second, column_place, column_count)
    share_plane = share_first[:, None] * share_second[None, :]
    live_vertical = (vertical_node_count >= 0).astype(jnp.float32)
    weight_cells = share_plane[:, :, None] * live_vertical[None, None, :]
    live_cells = (
        (nodes_first >= 0)[:, None, None]
        & (nodes_second >= 0)[None, :, None]
        & (vertical_node_count >= 0)[None, None, :]
    )
    load = assemble(jnp.where(live_cells, right_side, 0.0))
    diagonal = assemble(diagonal_local)
    inverse_diagonal = jnp.where(live_cells, 1.0 / jnp.where(live_cells, diagonal, 1.0), 0.0)
    blocks = coarse_factor.shape[0]
    block_depth = depth // blocks

    def coarse_terms(resid):
        per_level = jnp.einsum("xy,xyk->k", share_plane, resid, precision=HIGHEST)
        partial_value = jnp.sum(per_level.reshape(blocks, block_depth), axis=1)
        return jnp.dot(partial_value, coarse_factor, precision=HIGHEST)

    def coarse_solution_grid(through):
        values = jnp.dot(coarse_factor, through, precision=HIGHEST)
        return assemble(weight_cells * jnp.repeat(values, block_depth)[None, None, :])

    def precondition(resid):
        partial_value = coarse_terms(resid)
        jacobi = inverse_diagonal * resid
        through = lax.psum(partial_value, ("gx", "gy"))
        smoothed = jacobi + coarse_solution_grid(through)
        rho_value = inner(resid, smoothed, weight_cells)
        return (smoothed, rho_value)

    solution = jnp.zeros_like(load)
    resid = load
    smoothed, rho_now = precondition(resid)
    direction = smoothed
    for iteration in range(ITERS):
        total = mass * direction
        along_first = jnp.einsum("qs,syk->qyk", table_first, direction, precision=HIGHEST)
        total = total + jnp.einsum(
            "qs,qyk->syk", table_first, coef_first * along_first, precision=HIGHEST
        )
        along_second = jnp.einsum("qs,xsk->xqk", table_second, direction, precision=HIGHEST)
        total = total + jnp.einsum(
            "qs,xqk->xsk", table_second, coef_second * along_second, precision=HIGHEST
        )
        along_vertical = jnp.einsum("xyk,qk->xyq", direction, table_vertical, precision=HIGHEST)
        total = total + jnp.einsum(
            "xyq,qk->xyk", coef_vertical * along_vertical, table_vertical, precision=HIGHEST
        )
        image = assemble(total)
        step_size = rho_now / inner(direction, image, weight_cells)
        solution = solution + step_size * direction
        resid = resid - step_size * image
        if iteration + 1 < ITERS:
            smoothed, rho_next = precondition(resid)
            direction = smoothed + rho_next / rho_now * direction
            rho_now = rho_next
    return (solution, resid)


def solution(mesh):
    in_specs = (
        P("gx", "gy", None),
        P("gx", "gy", None),
        P("gx", "gy", None),
        P("gx"),
        P("gy"),
        P(("gx", "gy"), None),
    )
    out_specs = (P("gx", "gy", None), P("gx", "gy", None))
    return jax.shard_map(body, mesh=mesh, in_specs=in_specs, out_specs=out_specs, check_vma=False)
```

profile of v0, /device:TPU:1, one launch (start us, length us, event | category | flops | bytes accessed | tf_op | source)
XLA Modules:
  0.0 1080.5 jit_solution(1355978463199004033)
XLA Ops:
  10.2 2.8 copy.56
  19.5 4.6 collective-permute-start.4
  25.4 1.9 collective-permute-start
  27.8 4.0 collective-permute-done
  32.5 2.1 collective-permute-start.1
  34.6 3.0 collective-permute-done.1
  43.6 2.1 collective-permute-done.3
  48.0 1.8 convolution_bitcast_fusion.13
  53.9 106.0 %psum.63 = f32[8192]{0:T(1024)} all-reduce(f32[8192]{0:T(1024)} %bitcast.202), channel_id=1, replica_groups=mesh['gx'=16,'gy'=32] {'gx','gy'}, use_global_device_ids=true, to_apply=%region_7.8 | all-reduce | flops 8192 | bytes 65536 | tf_op jit(solution)/shard_map/psum | solution.py:189
  164.4 4.1 collective-permute-start.8
  169.2 1.9 collective-permute-start.5
  171.1 1.9 collective-permute-start.9
  174.2 2.1 collective-permute-start.6
  176.4 2.0 collective-permute-start.10
  183.8 1.9 scatter-add.124
  187.0 1.7 scatter-add.125
  188.6 1.7 multiply_add_fusion.5
  197.4 4.2 collective-permute-start.12
  202.5 1.9 collective-permute-start.13
  204.4 3.7 collective-permute-done.13
  208.1 3.6 collective-permute-start.14
  214.6 1.7 scatter-add.130
  216.3 2.2 collective-permute-done.15
  221.7 2.3 fusion.17
  223.9 108.6 %all-reduce = (f32[]{:T(128)}, f32[]{:T(128)}) all-reduce(f32[]{:T(128)} %get-tuple-element.387, f32[]{:T(128)} %get-tuple-element.386), channel_id=1, replica_groups=mesh['gx'=16,'gy'=32] {'gx','gy'}, use_global_device_ids=true, to_apply=%region_9.10 | all-reduce | flops 2 | bytes 16 | tf_op jit(solution)/shard_map/psum | solution.py:112
  341.6 94.9 %psum.66 = f32[8192]{0:T(1024)} all-reduce(f32[8192]{0:T(1024)} %bitcast.204), channel_id=1, replica_groups=mesh['gx'=16,'gy'=32] {'gx','gy'}, use_global_device_ids=true, to_apply=%region_13.14 | all-reduce | flops 8192 | bytes 65536 | tf_op jit(solution)/shard_map/psum | solution.py:189
  441.1 2.5 collective-permute-start.16
  444.5 1.9 collective-permute-start.17
  446.4 3.7 collective-permute-done.17
  450.1 3.7 collective-permute-start.18
  456.8 1.7 scatter-add.136
  458.5 2.0 collective-permute-done.19
  463.7 2.2 fusion.19
  465.9 101.0 %psum.67 = f32[]{:T(128)} all-reduce(f32[]{:T(128)} %fusion.19), channel_id=1, replica_groups=mesh['gx'=16,'gy'=32] {'gx','gy'}, use_global_device_ids=true, to_apply=%region_15.16 | all-reduce | flops 1 | bytes 8 | tf_op jit(solution)/shard_map/psum | solution.py:112
  568.3 1.9 multiply_add_fusion.3
  577.3 3.3 collective-permute-start.20
  581.4 1.9 collective-permute-start.21
  583.3 3.7 collective-permute-done.21
  587.1 2.4 collective-permute-start.22
  592.3 1.7 scatter-add.144
  594.0 2.2 collective-permute-done.23
  599.4 2.0 fusion.21
  601.4 103.0 %psum.68 = f32[]{:T(128)} all-reduce(f32[]{:T(128)} %fusion.21), channel_id=1, replica_groups=mesh['gx'=16,'gy'=32] {'gx','gy'}, use_global_device_ids=true, to_apply=%region_17.18 | all-reduce | flops 1 | bytes 8 | tf_op jit(solution)/shard_map/psum | solution.py:112
  711.9 1.7 fusion.96
  713.6 95.2 %psum.69 = f32[8192]{0:T(1024)} all-reduce(f32[8192]{0:T(1024)} %bitcast.206), channel_id=1, replica_groups=mesh['gx'=16,'gy'=32] {'gx','gy'}, use_global_device_ids=true, to_apply=%region_19.20 | all-reduce | flops 8192 | bytes 65536 | tf_op jit(solution)/shard_map/psum | solution.py:189
  813.3 3.1 collective-permute-start.24
  817.3 1.9 collective-permute-start.25
  819.2 3.7 collective-permute-done.25
  822.9 3.2 collective-permute-start.26
  828.9 1.7 scatter-add.150
  830.6 2.2 collective-permute-done.27
  836.0 2.5 fusion.23
  838.5 101.4 %psum.70 = f32[]{:T(128)} all-reduce(f32[]{:T(128)} %fusion.23), channel_id=1, replica_groups=mesh['gx'=16,'gy'=32] {'gx','gy'}, use_global_device_ids=true, to_apply=%region_21.22 | all-reduce | flops 1 | bytes 8 | tf_op jit(solution)/shard_map/psum | solution.py:112
  941.2 1.9 multiply_add_fusion.1
  950.3 3.1 collective-permute-start.28
  954.3 1.9 collective-permute-start.29
  956.2 3.7 collective-permute-done.29
  959.9 2.6 collective-permute-start.30
  964.8 1.7 scatter-add.156
  966.4 1.9 collective-permute-done.31
  969.2 1.7 scatter-add.159
  970.9 2.2 fusion.25
  973.1 103.2 %psum.71 = f32[]{:T(128)} all-reduce(f32[]{:T(128)} %fusion.25), channel_id=1, replica_groups=mesh['gx'=16,'gy'=32] {'gx','gy'}, use_global_device_ids=true, to_apply=%region_23.24 | all-reduce | flops 1 | bytes 8 | tf_op jit(solution)/shard_map/psum | solution.py:112
  1077.7 2.6 multiply_subtract_fusion
  (367 shorter events, 117.5 us)
Async XLA Ops:
  0.6 51.7 %copy-start = (f32[16,8192]{1,0:T(8,128)S(1)}, f32[16,8192]{1,0:T(8,128)}, u32[]{:S(2)}) copy-start(f32[16,8192]{1,0:T(8,128)} %param.87) | copy-start | bytes 1572868
  0.7 14.8 %copy-start.52 = (s32[128]{0:T(128)}, s32[128]{0:T(128)S(1)}, u32[]{:S(2)}) copy-start(s32[128]{0:T(128)S(1)} %compare_select_fusion) | copy-start | bytes 1540
  1.4 16.2 %copy-start.40 = (s32[29]{0:T(128)}, s32[29]{0:T(128)S(1)}, u32[]{:S(2)}) copy-start(s32[29]{0:T(128)S(1)} %compare_select_fusion.1) | copy-start | bytes 352
  1.4 22.6 %copy-start.44 = (pred[29]{0:T(512)(128)(4,1)}, pred[29]{0:T(512)(128)(4,1)S(1)}, u32[]{:S(2)}) copy-start(pred[29]{0:T(512)(128)(4,1)S(1)} %broadcast_compare_fusion.3) | copy-start | bytes 91
  2.1 14.7 %copy-start.48 = (s32[43]{0:T(128)}, s32[43]{0:T(128)S(1)}, u32[]{:S(2)}) copy-start(s32[43]{0:T(128)S(1)} %compare_select_fusion.2) | copy-start | bytes 520
  2.1 21.9 %copy-start.57 = (pred[43]{0:T(512)(128)(4,1)}, pred[43]{0:T(512)(128)(4,1)S(1)}, u32[]{:S(2)}) copy-start(pred[43]{0:T(512)(128)(4,1)S(1)} %broadcast_compare_fusion.4) | copy-start | bytes 133
  10.2 2.9 copy-start.36
  10.2 3.0 copy-start.95
  10.2 4.6 copy-start.65
  10.2 4.6 copy-start.90
  14.7 2.9 copy-start.8
  14.8 2.8 copy-start.18
  15.0 2.7 copy-start.23
  15.0 2.7 copy-start.69
  15.0 2.6 copy-start.81
  15.4 2.3 copy-start.27
  15.4 2.3 copy-start.73
  17.7 6.5 copy-start.31
  19.5 149.0 %collective-permute-start.4 = (f32[1,29,128]{2,1,0:T(8,128)}, f32[1,29,128]{2,1,0:T(8,128)}, u32[]{:S(2)}, u32[]{:S(2)}) collective-permute-start(f32[1,29,128]{2,1,0:T(8,128)} %slice.823), channel_id=1, source_target_pairs={{0,32},{32,64},{64,96},{96,128},{128,160},{160,192},{192,224},{224... | collective-permute-start | bytes 44552 | tf_op jit(solution)/shard_map/ppermute | solution.py:21
  25.4 6.4 collective-permute-start
  32.5 5.0 collective-permute-start.1
  37.6 2.6 collective-permute-start.2
  40.9 4.8 collective-permute-start.3
  47.9 126.3 %copy-start.4 = (f32[43,29,128]{2,1,0:T(8,128)}, f32[43,29,128]{2,1,0:T(8,128)S(1)}, u32[]{:S(2)}) copy-start(f32[43,29,128]{2,1,0:T(8,128)S(1)} %scatter-add.111) | copy-start | bytes 1915396
  164.4 6.7 collective-permute-start.8
  169.2 5.0 collective-permute-start.5
  171.1 5.3 collective-permute-start.9
  174.2 4.2 collective-permute-start.6
  176.4 3.5 collective-permute-start.10
  178.6 4.5 collective-permute-start.7
  180.9 5.2 collective-permute-start.11
  183.8 279.9 %copy-start.3 = (f32[43,29,128]{2,1,0:T(8,128)}, f32[43,29,128]{2,1,0:T(8,128)S(1)}, u32[]{:S(2)}) copy-start(f32[43,29,128]{2,1,0:T(8,128)S(1)} %scatter-add.119) | copy-start | bytes 1915396
  197.4 5.1 collective-permute-start.12
  202.5 5.6 collective-permute-start.13
  208.1 4.6 copy-start.12
  208.1 4.5 collective-permute-start.14
  213.3 5.1 collective-permute-start.15
  333.8 2.3 copy-start.32
  441.1 3.4 collective-permute-start.16
  444.5 5.6 collective-permute-start.17
  450.1 4.6 copy-start.14
  450.1 4.6 collective-permute-start.18
  455.4 5.1 collective-permute-start.19
  577.3 4.1 collective-permute-start.20
  581.4 5.6 collective-permute-start.21
  587.0 3.4 copy-start.13
  587.1 3.3 collective-permute-start.22
  591.0 5.1 collective-permute-start.23
  705.7 2.3 copy-start.33
  813.3 3.9 collective-permute-start.24
  817.3 5.6 collective-permute-start.25
  822.9 4.1 copy-start.15
  822.9 4.1 collective-permute-start.26
  827.6 5.1 collective-permute-start.27
  943.1 6.0 copy-start.1
  949.1 21.8 %copy-start.22 = (f32[43,29]{1,0:T(8,128)S(1)}, f32[43,29]{1,0:T(8,128)}, u32[]{:S(2)}) copy-start(f32[43,29]{1,0:T(8,128)} %get-tuple-element.422) | copy-start | bytes 14968
  949.1 21.8 %copy-start.56 = (f32[128]{0:T(128)S(1)}, f32[128]{0:T(128)}, u32[]{:S(2)}) copy-start(f32[128]{0:T(128)} %fusion.104) | copy-start | bytes 1540
  950.3 127.4 %copy-start.2 = (f32[43,29,128]{2,1,0:T(8,128)S(1)}, f32[43,29,128]{2,1,0:T(8,128)}, u32[]{:S(2)}) copy-start(f32[43,29,128]{2,1,0:T(8,128)} %copy-done.1) | copy-start | bytes 1915396
  950.3 127.4 %copy-start.6 = (f32[43,29,128]{2,1,0:T(8,128)S(1)}, f32[43,29,128]{2,1,0:T(8,128)}, u32[]{:S(2)}) copy-start(f32[43,29,128]{2,1,0:T(8,128)} %copy-done.5) | copy-start | bytes 1915396
  950.3 3.9 collective-permute-start.28
  954.3 5.6 collective-permute-start.29
  959.9 3.6 copy-start.16
  959.9 3.5 collective-permute-start.30
  963.5 4.8 collective-permute-start.31
  (64 other events, 100.9 us)
where the time goes:
time: 1090 us; the launch traced here: 1080 us
  blocking collectives  813 us (75%)
  starting transfers between devices  73.4 us (7%)
  other arithmetic  51.2 us (5%)
  waiting for transfers between devices  49.2 us (5%)
  matrix products  41.4 us (4%)
  local copies, waits for them, and re-layouts  41 us (4%)
  between operations  10.9 us (1%)
    psum x5, blocking collectives, inner(): return lax.psum(jnp.sum(weight_cells * first * second), ('gx', 'gy'))  517 us
    psum x3, blocking collectives, precondition(): through = lax.psum(partial_value, ('gx', 'gy'))  296 us
    ppermute x16, starting transfers between devices, padded(): lax.ppermute(tail, axis, [(i, (i + 1) % count) for i in range(ends)])  47.5 us
    ppermute x16, waiting for transfers between devices, padded(): lax.ppermute(head, axis, [((i + 1) % count, i) for i in range(ends)])  36.5 us
    ppermute x16, starting transfers between devices, padded(): lax.ppermute(head, axis, [((i + 1) % count, i) for i in range(ends)])  25.9 us
    scatter-add x16, local copies, waits for them, and re-layouts, assemble(): result = result.at[:, 0].add(beside[:, 0]).at[:, -1].add(beside[:, -1])  22.4 us
  transfers between devices with their start and end apart: 32, of which 26 were waited for; matrix products, arithmetic and copies ran while one was open for 3% of the time, Pallas kernels for 0%

commit v1 on v0

v1 whole, which is shorter than its diff:
```python
import functools

import jax
import jax.numpy as jnp
import ml_dtypes
import numpy as np
from jax import lax
from jax.experimental import pallas as pl
from jax.experimental.pallas import tpu as pltpu
from jax.sharding import PartitionSpec as P

ITERS = 3
HIGHEST = lax.Precision.HIGHEST
MESH = pl.DeviceIdType.MESH
LANES = 128
ROWS = 32
PLANES = 48
DIRECTIONS = [(1, 0), (-1, 0), (0, 1), (0, -1), (1, 1), (1, -1), (-1, 1), (-1, -1)]


def gll_weights():
    return np.array(
        [
            1.0 / 28.0,
            0.2107042271435061,
            0.3411226924835044,
            0.4124587946587038,
            0.4124587946587038,
            0.3411226924835044,
            0.2107042271435061,
            1.0 / 28.0,
        ]
    )


def gll_derivative():
    points = np.array(
        [
            -1.0,
            -0.8717401485096066,
            -0.5917001814331423,
            -0.2092992179024789,
            0.2092992179024789,
            0.5917001814331423,
            0.8717401485096066,
            1.0,
        ]
    )
    identity = np.eye(8) > 0
    spacing = np.where(identity, 1.0, points[:, None] - points[None, :])
    barycentric = 1.0 / np.prod(spacing, axis=1)
    matrix = np.where(identity, 0.0, barycentric[None, :] / barycentric[:, None] / spacing)
    return np.where(identity, -np.sum(matrix, axis=1)[:, None], matrix)


WEIGHTS = gll_weights()
STIFF = gll_derivative().T @ np.diag(WEIGHTS) @ gll_derivative()


def split(matrix):
    high = matrix.astype(ml_dtypes.bfloat16)
    low = (matrix - high.astype(np.float64)).astype(ml_dtypes.bfloat16)
    return high, low


def band(cells, size):
    first, second = np.zeros((size, size)), np.zeros((size, size))
    for e in range(cells):
        for b in range(7):
            first[7 * e + b, 7 * e : 7 * e + 8] = STIFF[b]
        second[7 * e + 7, 7 * e : 7 * e + 8] = STIFF[7]
    return first, second


def tables(cap_x, cap_y, layers):
    first, second = band(layers, LANES)
    high, low = split(np.concatenate([first, second], axis=0).T)
    vertical = np.concatenate([high, high, low], axis=0)
    first, second = band(cap_y, ROWS)
    stacked = np.concatenate([np.kron(np.eye(4), first), np.kron(np.eye(4), second)], axis=0)
    high, low = split(stacked)
    across = np.concatenate([high, high, low], axis=1)
    depth = np.zeros((LANES, 3 * LANES))
    for h in range(layers):
        depth[h, 7 * h : 7 * h + 8] = WEIGHTS
        depth[h, LANES + 7 * h : LANES + 7 * h + 7] = 1.0
        depth[h, 2 * LANES + 7 * h + 7] = 1.0
    weigh, pick, ends = np.zeros((ROWS, 8)), np.zeros((ROWS, 8)), np.zeros((ROWS, 8))
    for f in range(cap_y):
        weigh[7 * f : 7 * f + 8, f] = WEIGHTS
        pick[7 * f : 7 * f + 7, f] = 1.0
        ends[7 * f + 7, f] = 1.0
    unit = np.eye(cap_x)
    widen = np.concatenate([np.kron(unit, weigh), np.kron(unit, pick), np.kron(unit, ends)], axis=0)
    widen = np.pad(widen, ((0, 0), (0, LANES - widen.shape[1])))
    factor = np.zeros((ROWS + 8, LANES))
    factor[: 7 * cap_y] = STIFF[np.arange(7 * cap_y) % 7, np.arange(7 * cap_y) % 7][:, None]
    factor[ROWS:, : 7 * layers] = STIFF[np.arange(7 * layers) % 7, np.arange(7 * layers) % 7][None, :]
    return (
        vertical,
        across,
        depth.astype(np.float32),
        widen.astype(np.float32),
        factor.astype(np.float32),
    )


def plane(x):
    return pl.ds(pl.multiple_of(x * ROWS, ROWS), ROWS)


def total(values):
    return jnp.sum(values, axis=(0, 1), keepdims=True)


def iota(shape, dim):
    return lax.broadcasted_iota(jnp.int32, shape, dim)


def kernel(
    nx, ny, cap_x, cap_y, layers,
    wx_ref, wy_ref, load_ref, diff_ref, kappa_ref, factor_ref,
    vertical_ref, across_ref, depth_ref, widen_ref, coefficient_ref,
    solution_ref, residual_ref,
    f_d, f_im, f_r, f_sol, f_inv, f_wid, f_mass, f_ya, f_yb, f_za, f_zb,
    e_px, e_big, e_ya, e_yb, squares, sq_kappa, t_now,
    halo_sx, halo_sy, halo_sc, halo_rx, halo_ry, halo_rc,
    coarse_s, coarse_r, part, recv1, msg2, recv2, msg3, recv3,
    last_s, last_r, last_s3, last_r3,
    h_send, h_recv, c_send, c_recv, r_send, r_recv, l_send, l_recv,
):
    p, q = lax.axis_index("gx"), lax.axis_index("gy")
    wx, wy = wx_ref[0], wy_ref[0]
    groups = part.shape[2]
    end_x, end_y = 7 * wx, 7 * wy

    def beside(dx, dy):
        return (lax.rem(p + dx + nx, nx), lax.rem(q + dy + ny, ny))

    barrier = pltpu.get_barrier_semaphore()

    def greet_gx(o, _):
        pl.semaphore_signal(barrier, inc=1, device_id=beside(o, 0), device_id_type=MESH)
        return 0

    def greet_gy(o, _):
        pl.semaphore_signal(barrier, inc=1, device_id=beside(0, o), device_id_type=MESH)
        return 0

    lax.fori_loop(1, nx, greet_gx, 0)
    lax.fori_loop(1, ny, greet_gy, 0)
    for dx, dy in DIRECTIONS[4:]:
        pl.semaphore_signal(barrier, inc=1, device_id=beside(dx, dy), device_id_type=MESH)

    def flag(condition):
        return jnp.where(condition, 1.0, 0.0).astype(jnp.float32)

    has_left, has_right = flag(p > 0), flag(p < nx - 1)
    has_below, has_above = flag(q > 0), flag(q < ny - 1)

    squares[...] = jnp.zeros_like(squares)
    sq_kappa[...] = jnp.zeros_like(sq_kappa)
    inside = iota((cap_y, layers), 0) < wy
    for e in range(cap_x):
        keep = inside & (e < wx)
        squares[8 * e : 8 * e + cap_y, 0:layers] = jnp.where(keep, diff_ref[e], 0.0)
        sq_kappa[8 * e : 8 * e + cap_y, 0:layers] = jnp.where(keep, kappa_ref[e], 0.0)
    deep = jnp.dot(squares[...], depth_ref[...], precision=HIGHEST, preferred_element_type=jnp.float32)
    deep_kappa = jnp.dot(
        sq_kappa[...], depth_ref[:, 0:LANES], precision=HIGHEST, preferred_element_type=jnp.float32
    )
    tall = cap_x * ROWS
    big = jnp.dot(
        widen_ref[0:tall, :],
        jnp.concatenate([deep, deep_kappa], axis=1),
        precision=HIGHEST,
        preferred_element_type=jnp.float32,
    )
    both = jnp.dot(
        widen_ref[tall : 3 * tall, :],
        deep[:, 0:LANES],
        precision=HIGHEST,
        preferred_element_type=jnp.float32,
    )
    zero_plane = jnp.zeros((ROWS, LANES), jnp.float32)
    for ref in (e_px, e_ya, e_yb):
        ref[0:ROWS, :] = zero_plane
        ref[tall + ROWS : tall + 2 * ROWS, :] = zero_plane
    for place in (0, tall + ROWS):
        e_big[place : place + ROWS, :] = jnp.zeros((ROWS, 3 * LANES), jnp.float32)
    e_px[ROWS : ROWS + tall, :] = big[:, 0:LANES]
    e_big[ROWS : ROWS + tall, :] = big[:, LANES : 4 * LANES]
    e_ya[ROWS : ROWS + tall, :] = both[0:tall]
    e_yb[ROWS : ROWS + tall, :] = both[tall : 2 * tall]

    for ref in (f_d, f_im, f_r, f_inv, f_wid, f_mass, f_ya, f_yb, f_za, f_zb):
        for x in range(7 * cap_x, PLANES):
            ref[x * ROWS : (x + 1) * ROWS, :] = zero_plane

    sources = (
        (f_za, e_big, 0), (f_zb, e_big, 1), (f_mass, e_big, 2), (f_ya, e_ya, 0), (f_yb, e_yb, 0),
    )
    row_factor = coefficient_ref[0:ROWS, :]
    depth_factor = coefficient_ref[ROWS : ROWS + 1, :]
    corner = float(STIFF[7, 7])

    def fill_plane(x, e, b):
        values = []
        for target, source, lane in sources:
            lanes = slice(lane * LANES, (lane + 1) * LANES)
            value = float(WEIGHTS[b]) * source[plane(e + 1), lanes]
            if b == 0:
                value = value + float(WEIGHTS[7]) * source[plane(e), lanes]
            target[plane(x), :] = value
            values.append(value)
        za, zb, mass, ya, yb = values
        diagonal = mass + ya * row_factor + yb * corner + za * depth_factor + zb * corner
        diagonal = diagonal + float(STIFF[b, b]) * e_px[plane(e + 1), :]
        if b == 0:
            diagonal = diagonal + float(STIFF[7, 7]) * e_px[plane(e), :]
        f_inv[plane(x), :] = diagonal

    def fill(e, _):
        for b in range(7):
            fill_plane(7 * e + b, e, b)
        return 0

    lax.fori_loop(0, cap_x, fill, 0)
    fill_plane(7 * cap_x, cap_x, 0)

    slots_x, slots_y = load_ref.shape[0], load_ref.shape[1]
    row = iota((slots_y, LANES), 0)
    real = iota((slots_y, LANES), 1) <= 7 * layers
    f_r[...] = jnp.zeros_like(f_r)

    def take(x, _):
        value = jnp.where(x < end_x, load_ref[x], jnp.where(x == end_x, load_ref[slots_x - 1], 0.0))
        last = value[slots_y - 1 : slots_y, :]
        value = jnp.where(row < end_y, value, jnp.where(row == end_y, last, 0.0))
        f_r[pl.ds(pl.multiple_of(x * ROWS, ROWS), slots_y), :] = jnp.where(real, value, 0.0)
        return 0

    lax.fori_loop(0, slots_x, take, 0)

    def high_plane(ref):
        value = jnp.zeros((ROWS, LANES), jnp.float32)
        for j in range(1, cap_x + 1):
            value = value + jnp.where(wx == j, ref[7 * j * ROWS : (7 * j + 1) * ROWS, :], 0.0)
        return value

    def side(j):
        return pl.ds(7 * j, PLANES, stride=ROWS)

    def high_row(plane_value):
        value = jnp.zeros((1, LANES), jnp.float32)
        for j in range(1, cap_y + 1):
            value = value + jnp.where(wy == j, plane_value[7 * j : 7 * j + 1, :], 0.0)
        return value

    def remote(source, target, send, recv, device):
        return pltpu.make_async_remote_copy(
            src_ref=source,
            dst_ref=target,
            send_sem=send,
            recv_sem=recv,
            device_id=device,
            device_id_type=MESH,
        )

    def halo_copies(h):
        copies = []
        for k, (dx, dy) in enumerate(DIRECTIONS):
            if dy == 0:
                slot = (h, 0 if dx > 0 else 1)
                source, target = halo_sx.at[slot], halo_rx.at[slot]
            elif dx == 0:
                slot = (h, 0 if dy > 0 else 1)
                source, target = halo_sy.at[slot], halo_ry.at[slot]
            else:
                source, target = halo_sc.at[h, k - 4], halo_rc.at[h, k - 4]
            copies.append(remote(source, target, h_send.at[h, k], h_recv.at[h, k], beside(dx, dy)))
        return copies

    def halo_start(h, ref):
        low, high = ref[0:ROWS, :], high_plane(ref)
        halo_sx[h, 0] = high
        halo_sx[h, 1] = low
        above = jnp.zeros((PLANES, LANES), jnp.float32)
        for j in range(1, cap_y + 1):
            above = above + jnp.where(wy == j, ref[side(j), :], 0.0)
        halo_sy[h, 0] = above
        halo_sy[h, 1] = ref[side(0), :]
        rows = (high_row(high), high[0:1, :], high_row(low), low[0:1, :])
        for k, value in enumerate(rows):
            halo_sc[h, k] = jnp.broadcast_to(value, (8, LANES))
        copies = halo_copies(h)
        for copy in copies:
            copy.start()
        return copies

    place = iota((PLANES, LANES), 0)

    def halo_finish(h, ref, copies):
        for copy in copies:
            copy.wait()
        ref[0:ROWS, :] = ref[0:ROWS, :] + has_left * halo_rx[h, 0]
        from_right = has_right * halo_rx[h, 1]
        for j in range(1, cap_x + 1):
            rows = slice(7 * j * ROWS, (7 * j + 1) * ROWS)
            ref[rows, :] = ref[rows, :] + jnp.where(wx == j, from_right, 0.0)

        def line(side_value, near, far):
            side_value = side_value + jnp.where(place == 0, has_left * near[0:1, :], 0.0)
            return side_value + jnp.where(place == end_x, has_right * far[0:1, :], 0.0)

        below = has_below * line(halo_ry[h, 0], halo_rc[h, 0], halo_rc[h, 2])
        above = has_above * line(halo_ry[h, 1], halo_rc[h, 1], halo_rc[h, 3])
        ref[side(0), :] = ref[side(0), :] + below
        for j in range(1, cap_y + 1):
            ref[side(j), :] = ref[side(j), :] + jnp.where(wy == j, above, 0.0)

    pl.semaphore_wait(barrier, nx + ny + 2)
    load_copies = halo_start(0, f_r)
    diagonal_copies = halo_start(1, f_inv)
    halo_finish(0, f_r, load_copies)

    row32 = iota((ROWS, LANES), 0)
    share_low = jnp.where(row32 == 0, 1.0 - 0.5 * has_below, 1.0)
    share_row = jnp.where(row32 == end_y, 1.0 - 0.5 * has_above, share_low)
    block = LANES // 16

    def share_x(x):
        low = jnp.where(x == 0, 1.0 - 0.5 * has_left, 1.0)
        return jnp.where(x == end_x, 1.0 - 0.5 * has_right, low)

    chunk = 4 * ROWS
    chunks = (7 * cap_x + 4) // 4

    def coarse_sums(ref):
        def add(i, value):
            return value + jnp.sum(
                ref[pl.ds(pl.multiple_of(i * chunk, chunk), chunk), :].reshape(4, ROWS, LANES), axis=0
            )

        value = lax.fori_loop(0, chunks, add, jnp.zeros((ROWS, LANES), jnp.float32))
        value = value - 0.5 * has_left * ref[0:ROWS, :] - 0.5 * has_right * high_plane(ref)
        return jnp.sum(share_row * value, axis=0, keepdims=True)

    def reduce_start(a, ref):
        profile = coarse_sums(ref)
        mask = iota((16, LANES), 1) // block == iota((16, LANES), 0)
        column = jnp.sum(jnp.where(mask, profile, 0.0), axis=1, keepdims=True)
        for i in range(nx):
            for g in range(groups):
                lanes = slice((i * groups + g) * LANES, (i * groups + g + 1) * LANES)
                part[a, i, g : g + 1, :] = jnp.sum(factor_ref[:, lanes] * column, axis=0, keepdims=True)

        def send(o, _):
            peer = lax.rem(p + o, nx)
            remote(
                part.at[a, peer], recv1.at[a, p], r_send.at[a, 0], r_recv.at[a, 0], (peer, q)
            ).start()
            return 0

        lax.fori_loop(1, nx, send, 0)
        recv1[a, p] = part[a, p]

    def wait_in(buffer, count, send, recv, device):
        remote(buffer.at[pl.ds(0, count)], buffer.at[pl.ds(0, count)], send, recv, device).wait_recv()

    def wait_out(buffer, count, send, recv, device):
        remote(buffer.at[pl.ds(0, count)], buffer.at[pl.ds(0, count)], send, recv, device).wait_send()

    lane = iota((1, LANES), 1)

    def scalar_row(values):
        result = jnp.zeros((1, LANES), jnp.float32)
        for i, value in enumerate(values):
            result = jnp.where(lane == i, value, result)
        return result

    def pick(values, i):
        return total(jnp.where(lane == i, values, 0.0))

    def reduce_finish(a, scalars):
        wait_in(recv1.at[a], nx - 1, r_send.at[a, 0], r_recv.at[a, 0], beside(1, 0))
        msg2[a, 0:groups, :] = jnp.sum(recv1[a], axis=0)
        msg2[a, groups : groups + 1, :] = scalar_row(scalars)

        def send2(o, _):
            peer = lax.rem(q + o, ny)
            remote(
                msg2.at[a], recv2.at[a, q], r_send.at[a, 1], r_recv.at[a, 1], (p, peer)
            ).start()
            return 0

        lax.fori_loop(1, ny, send2, 0)
        recv2[a, q] = msg2[a]
        wait_in(recv2.at[a], ny - 1, r_send.at[a, 1], r_recv.at[a, 1], beside(0, 1))
        msg3[a] = jnp.sum(recv2[a], axis=0)

        def send3(o, _):
            peer = lax.rem(p + o, nx)
            remote(
                msg3.at[a], recv3.at[a, p], r_send.at[a, 2], r_recv.at[a, 2], (peer, q)
            ).start()
            return 0

        lax.fori_loop(1, nx, send3, 0)
        recv3[a, p] = msg3[a]
        wait_in(recv3.at[a], nx - 1, r_send.at[a, 2], r_recv.at[a, 2], beside(1, 0))
        sums = jnp.sum(recv3[a, :, groups : groups + 1, :], axis=0)
        wait_out(recv1.at[a], nx - 1, r_send.at[a, 0], r_recv.at[a, 0], beside(1, 0))
        wait_out(recv2.at[a], ny - 1, r_send.at[a, 1], r_recv.at[a, 1], beside(0, 1))
        wait_out(recv3.at[a], nx - 1, r_send.at[a, 2], r_recv.at[a, 2], beside(1, 0))
        return sums

    def coarse_start(a):
        value = jnp.zeros((16, LANES), jnp.float32)
        for i in range(nx):
            for g in range(groups):
                lanes = slice((i * groups + g) * LANES, (i * groups + g + 1) * LANES)
                value = value + factor_ref[:, lanes] * t_now[i, g : g + 1, :]
        column = jnp.sum(value, axis=1, keepdims=True)
        mask = iota((16, LANES), 1) // block == iota((16, LANES), 0)
        values = jnp.sum(jnp.where(mask, column, 0.0), axis=0, keepdims=True)
        coarse_s[a] = jnp.broadcast_to(values, (8, LANES))
        copies = []
        for k, (dx, dy) in enumerate(DIRECTIONS):
            copy = remote(
                coarse_s.at[a], coarse_r.at[a, k], c_send.at[a, k], c_recv.at[a, k], beside(dx, dy)
            )
            copy.start()
            copies.append(copy)
        return copies

    def next_direction(a, copies, beta):
        for copy in copies:
            copy.wait()
        own = coarse_s[a, 0:1, :]
        got = {step: coarse_r[a, k, 0:1, :] for k, step in enumerate(DIRECTIONS)}
        got[(0, 0)] = own

        def spread(dx):
            centre, low, high = got[(dx, 0)], got[(dx, 1)], got[(dx, -1)]
            value = jnp.where(row32 == 0, centre + 0.5 * has_below * (low - centre), centre)
            return jnp.where(row32 == end_y, value + 0.5 * has_above * (high - centre), value)

        middle = spread(0)
        near = middle + 0.5 * has_left * (spread(1) - middle)
        far = middle + 0.5 * has_right * (spread(-1) - middle)

        def update(x, _):
            inv = f_inv[plane(x), :]
            coarse = jnp.where(x == 0, near, jnp.where(x == end_x, far, middle))
            value = inv * f_r[plane(x), :] + jnp.where(inv > 0.0, coarse, 0.0)
            if beta is not None:
                value = value + beta * f_d[plane(x), :]
            f_d[plane(x), :] = value
            return 0

        lax.fori_loop(0, 7 * cap_x + 1, update, 0)

    def apply_operator():
        def along_x(e, carried):
            values = [f_d[plane(7 * e + c), :] for c in range(8)]
            sums = [values[c] + values[7 - c] for c in range(4)]
            gaps = [values[c] - values[7 - c] for c in range(4)]
            scale = e_px[plane(e + 1), :]
            results = [None] * 8
            for b in range(4):
                even = sum(float(0.5 * (STIFF[b, c] + STIFF[b, 7 - c])) * sums[c] for c in range(4))
                odd = sum(float(0.5 * (STIFF[b, c] - STIFF[b, 7 - c])) * gaps[c] for c in range(4))
                results[b] = scale * (even + odd)
                results[7 - b] = scale * (even - odd)
            f_im[plane(7 * e), :] = carried + results[0]
            for b in range(1, 7):
                f_im[plane(7 * e + b), :] = results[b]
            return results[7]

        carried = lax.fori_loop(0, cap_x, along_x, zero_plane)
        f_im[plane(7 * cap_x), :] = carried

        def along_rest(i, product):
            rows = pl.ds(pl.multiple_of(i * chunk, chunk), chunk)
            value = f_d[rows, :]
            high = value.astype(jnp.bfloat16)
            low = (value - high.astype(jnp.float32)).astype(jnp.bfloat16)
            deep = jnp.dot(
                jnp.concatenate([high, low, high], axis=1),
                vertical_ref[...],
                preferred_element_type=jnp.float32,
            )
            wide = jnp.dot(
                across_ref[...],
                jnp.concatenate([high, low, high], axis=0),
                preferred_element_type=jnp.float32,
            )
            image = f_im[rows, :] + f_mass[rows, :] * value
            image = image + f_ya[rows, :] * wide[0:chunk] + f_yb[rows, :] * wide[chunk:]
            image = image + f_za[rows, :] * deep[:, 0:LANES] + f_zb[rows, :] * deep[:, LANES:]
            f_im[rows, :] = image
            return product + jnp.sum((value * image).reshape(chunk // 8, 8, LANES), axis=0)

        product = lax.fori_loop(0, chunks, along_rest, jnp.zeros((8, LANES), jnp.float32))
        return total(product)

    step0 = reduce_start(0, f_r)
    del step0
    halo_finish(1, f_inv, diagonal_copies)

    def invert(x, value):
        diagonal = f_inv[plane(x), :]
        inverse = jnp.where(diagonal > 0.0, 1.0 / jnp.where(diagonal > 0.0, diagonal, 1.0), 0.0)
        f_inv[plane(x), :] = inverse
        weighed = inverse * share_row * share_x(x)
        f_wid[plane(x), :] = weighed
        resid = f_r[plane(x), :]
        f_sol[plane(x), :] = zero_plane
        return value + weighed * resid * resid

    jacobi = total(lax.fori_loop(0, 7 * cap_x + 1, invert, zero_plane))
    sums = reduce_finish(0, [jacobi])
    jacobi = pick(sums, 0)
    t_now[...] = recv3[0, :, 0:groups, :]
    rho = jacobi + total(jnp.sum(t_now[...] * t_now[...], axis=0))
    copies = coarse_start(0)
    next_direction(0, copies, None)

    for i in range(ITERS):
        curvature = apply_operator()
        image_copies = halo_start(2 + i, f_im)
        if i + 1 < ITERS:
            halo_finish(2 + i, f_im, image_copies)
            reduce_start(i + 1, f_im)

            def dots(x, values):
                image = f_im[plane(x), :]
                weighed = f_wid[plane(x), :] * image
                return (values[0] + weighed * f_r[plane(x), :], values[1] + weighed * image)

            cross, square = lax.fori_loop(0, 7 * cap_x + 1, dots, (zero_plane, zero_plane))
            sums = reduce_finish(i + 1, [curvature, total(cross), total(square)])
            step = rho / pick(sums, 0)
            cross, square = pick(sums, 1), pick(sums, 2)
            jacobi = jacobi - 2.0 * step * cross + step * step * square
            for k in range(nx):
                t_now[k] = t_now[k] - step * recv3[i + 1, k, 0:groups, :]
            rho_next = jacobi + total(jnp.sum(t_now[...] * t_now[...], axis=0))
            copies = coarse_start(i + 1)

            def advance(x, _):
                f_sol[plane(x), :] = f_sol[plane(x), :] + step * f_d[plane(x), :]
                f_r[plane(x), :] = f_r[plane(x), :] - step * f_im[plane(x), :]
                return 0

            lax.fori_loop(0, 7 * cap_x + 1, advance, 0)
            next_direction(i + 1, copies, rho_next / rho)
            rho = rho_next
        else:
            last_s[...] = jnp.broadcast_to(curvature, (1, LANES))

            def send_last(o, _):
                peer = lax.rem(q + o, ny)
                remote(last_s, last_r.at[q], l_send.at[0], l_recv.at[0], (p, peer)).start()
                return 0

            lax.fori_loop(1, ny, send_last, 0)
            last_r[q] = last_s[...]
            halo_finish(2 + i, f_im, image_copies)
            wait_in(last_r, ny - 1, l_send.at[0], l_recv.at[0], beside(0, 1))
            last_s3[...] = jnp.sum(last_r[...], axis=0)

            def send_end(o, _):
                peer = lax.rem(p + o, nx)
                remote(last_s3, last_r3.at[p], l_send.at[1], l_recv.at[1], (peer, q)).start()
                return 0

            lax.fori_loop(1, nx, send_end, 0)
            last_r3[p] = last_s3[...]
            wait_in(last_r3, nx - 1, l_send.at[1], l_recv.at[1], beside(1, 0))
            step = rho / jnp.sum(last_r3[...], axis=0)
            wait_out(last_r, ny - 1, l_send.at[0], l_recv.at[0], beside(0, 1))
            wait_out(last_r3, nx - 1, l_send.at[1], l_recv.at[1], beside(1, 0))

    def finish(x, _):
        f_sol[plane(x), :] = f_sol[plane(x), :] + step * f_d[plane(x), :]
        f_r[plane(x), :] = f_r[plane(x), :] - step * f_im[plane(x), :]
        return 0

    lax.fori_loop(0, 7 * cap_x + 1, finish, 0)

    def put(source, target, x, value):
        last = high_row(value)
        rows = value[0:slots_y, :]
        rows = jnp.where(row < end_y, rows, jnp.where(row == slots_y - 1, last, 0.0))
        target[x] = rows

    for source, target in ((f_sol, solution_ref), (f_r, residual_ref)):

        def write(x, _):
            put(source, target, x, jnp.where(x < end_x, source[plane(x), :], 0.0))
            return 0

        lax.fori_loop(0, slots_x - 1, write, 0)
        put(source, target, slots_x - 1, high_plane(source))


def body(nx, ny, right_side, diffusion, kappa, widths_x, widths_y, factor):
    cap_x, cap_y, layers = diffusion.shape
    slots_x, slots_y, depth = right_side.shape
    groups = factor.shape[1] // (nx * LANES)
    f32 = jnp.float32
    smem = pl.BlockSpec(memory_space=pltpu.SMEM)
    vmem = pl.BlockSpec(memory_space=pltpu.VMEM)
    tall = cap_x * ROWS
    field = pltpu.VMEM((PLANES * ROWS, LANES), f32)
    dma = pltpu.SemaphoreType.DMA
    scratch = [field] * 11 + [
        pltpu.VMEM((tall + 2 * ROWS, LANES), f32),
        pltpu.VMEM((tall + 2 * ROWS, 3 * LANES), f32),
        pltpu.VMEM((tall + 2 * ROWS, LANES), f32),
        pltpu.VMEM((tall + 2 * ROWS, LANES), f32),
        pltpu.VMEM((LANES, LANES), f32),
        pltpu.VMEM((LANES, LANES), f32),
        pltpu.VMEM((nx, groups, LANES), f32),
    ]
    halos = 2 + ITERS
    for _ in range(2):
        scratch += [
            pltpu.VMEM((halos, 2, ROWS, LANES), f32),
            pltpu.VMEM((halos, 2, PLANES, LANES), f32),
            pltpu.VMEM((halos, 4, 8, LANES), f32),
        ]
    scratch += [
        pltpu.VMEM((ITERS, 8, LANES), f32),
        pltpu.VMEM((ITERS, 8, 8, LANES), f32),
        pltpu.VMEM((ITERS, nx, groups, LANES), f32),
        pltpu.VMEM((ITERS, nx, groups, LANES), f32),
        pltpu.VMEM((ITERS, groups + 1, LANES), f32),
        pltpu.VMEM((ITERS, ny, groups + 1, LANES), f32),
        pltpu.VMEM((ITERS, groups + 1, LANES), f32),
        pltpu.VMEM((ITERS, nx, groups + 1, LANES), f32),
        pltpu.VMEM((1, LANES), f32),
        pltpu.VMEM((ny, 1, LANES), f32),
        pltpu.VMEM((1, LANES), f32),
        pltpu.VMEM((nx, 1, LANES), f32),
        dma((halos, 8)), dma((halos, 8)), dma((ITERS, 8)), dma((ITERS, 8)),
        dma((ITERS, 3)), dma((ITERS, 3)), dma((2,)), dma((2,)),
    ]
    shape = jax.ShapeDtypeStruct(right_side.shape, f32)
    constants = [jnp.asarray(table) for table in tables(cap_x, cap_y, layers)]
    return pl.pallas_call(
        functools.partial(kernel, nx, ny, cap_x, cap_y, layers),
        out_shape=(shape, shape),
        in_specs=[smem, smem] + [vmem] * 9,
        out_specs=(vmem, vmem),
        scratch_shapes=scratch,
        compiler_params=pltpu.CompilerParams(
            collective_id=0, has_side_effects=True, vmem_limit_bytes=48 * 1024 * 1024
        ),
    )(widths_x, widths_y, right_side, diffusion, kappa, factor, *constants)


def solution(mesh):
    nx, ny = mesh.shape["gx"], mesh.shape["gy"]
    in_specs = (
        P("gx", "gy", None),
        P("gx", "gy", None),
        P("gx", "gy", None),
        P("gx"),
        P("gy"),
        P(("gx", "gy"), None),
    )
    out_specs = (P("gx", "gy", None), P("gx", "gy", None))
    return jax.shard_map(
        functools.partial(body, nx, ny),
        mesh=mesh,
        in_specs=in_specs,
        out_specs=out_specs,
        check_vma=False,
    )
```

time: 1090 us -> 131 us (0.12)
  blocking collectives: 813 us -> 0 us
  Pallas kernels: 0 us -> 119 us
  starting transfers between devices: 73.4 us -> 0 us
  other arithmetic: 51.2 us -> 0 us
  waiting for transfers between devices: 49.2 us -> 0 us
  matrix products: 41.4 us -> 0 us
  local copies, waits for them, and re-layouts: 41 us -> 9.73 us
    psum x8 -> x0, blocking collectives: 813 us -> none  [the longest x5 517 us: inner(): return lax.psum(jnp.sum(weight_cells * first * second), ('gx', 'gy'))]
    pallas_call x0 -> x1, Pallas kernels: none -> 119 us  [body(): pl.pallas_call(functools.partial(kernel, nx, ny, cap_x, cap_y, layers), o...]
    ppermute x32 -> x0, starting transfers between devices: 73.4 us -> none  [the longest x16 47.5 us: padded(): lax.ppermute(tail, axis, [(i, (i + 1) % count) for i in range(ends)])]
    ppermute x32 -> x0, waiting for transfers between devices: 49.2 us -> none  [the longest x16 36.5 us: padded(): lax.ppermute(head, axis, [((i + 1) % count, i) for i in range(ends)])]
    dot_general x38 -> x0, matrix products: 41.4 us -> none  [the longest x3 4.9 us: coarse_terms(): return jnp.dot(partial_value, coarse_factor, precision=HIGHEST)]
    scatter-add x16 -> x0, local copies, waits for them, and re-layouts: 22.4 us -> none  [assemble(): result = result.at[:, 0].add(beside[:, 0]).at[:, -1].add(beside[:, -1])]
    reduce_sum x14 -> x0, other arithmetic: 18 us -> none  [the longest x5 11.3 us: inner(): return lax.psum(jnp.sum(weight_cells * first * second), ('gx', 'gy'))]
    add x11 -> x0, other arithmetic: 15 us -> none  [the longest x8 9.56 us: assemble(): result = result.at[:, 0].add(beside[:, 0]).at[:, -1].add(beside[:, -1])]
  transfers between devices with their start and end apart: 32 -> 0, of which waited for: 26 -> 0; matrix products, arithmetic and copies ran while one was open for 3% -> 0% of each run, Pallas kernels for 0% -> 0%
where the time goes in v1:
time: 131 us
  Pallas kernels  119 us (91%)
  local copies, waits for them, and re-layouts  9.73 us (7%)
  between operations  1.95 us (1%)
    pallas_call x1, Pallas kernels, body(): pl.pallas_call(functools.partial(kernel, nx, ny, cap_x, cap_y, layers), o...  119 us
    unnamed x20, local copies, waits for them, and re-layouts  9.73 us

profile of v1, /device:TPU:1, one launch (start us, length us, event | category | flops | bytes accessed | tf_op | source)
XLA Modules:
  0.0 130.7 jit_solution(16887020528946507769)
XLA Ops:
  1.9 0.0 copy-start
  1.9 1.1 copy-done
  3.0 0.0 copy-start.1
  3.0 1.0 copy-done.1
  4.1 0.0 copy-start.2
  4.1 1.0 copy-done.2
  5.0 0.0 copy-start.3
  5.0 0.9 copy-done.3
  6.0 0.0 copy-start.4
  6.0 0.9 copy-done.4
  6.9 0.0 copy-start.5
  6.9 0.9 copy-done.5
  7.8 0.0 copy-start.6
  7.8 0.7 copy-done.6
  8.5 0.0 copy-start.7
  8.5 0.7 copy-done.7
  9.2 0.0 copy-start.8
  9.3 0.7 copy-done.8
  10.0 119.0 %shard_map.122 = (f32[43,29,128]{2,1,0:T(8,128)S(1)}, f32[43,29,128]{2,1,0:T(8,128)S(1)}) custom-call(s32[1]{0:T(128)S(6)} %copy.15.wx_ref, s32[1]{0:T(128)S(6)} %copy.16.wy_ref, f32[43,29,128]{2,1,0:T(8,128)S(1)} %copy-done, f32[6,4,18]{2,1,0:T(4,128)S(1)} %copy-done.7, f32[6,4,18]{2,1,0:T(4,128)S(1)} %copy-done.8, f32[16,8192]{1,0:T(8,128)S(1)} %copy-done.1, ...), custom_call_target="tpu_custom_call" | custom-call | tf_op jit(solution)/shard_map/pallas_call | solution.py:653
  129.0 0.9 copy.17
  129.8 0.9 copy.18
Async XLA Ops:
  1.9 1.1 copy-start
  3.0 1.0 copy-start.1
  4.1 1.0 copy-start.2
  5.0 0.9 copy-start.3
  6.0 0.9 copy-start.4
  6.9 0.9 copy-start.5
  7.8 0.7 copy-start.6
  8.5 0.7 copy-start.7
  9.2 0.7 copy-start.8

commit v2 on v1

v2 whole, which is shorter than its diff:
```python
import functools

import jax
import jax.numpy as jnp
import ml_dtypes
import numpy as np
from jax import lax
from jax.experimental import pallas as pl
from jax.experimental.pallas import tpu as pltpu
from jax.sharding import PartitionSpec as P

ITERS = 3
HIGHEST = lax.Precision.HIGHEST
MESH = pl.DeviceIdType.MESH
LANES = 128
ROWS = 32
PLANES = 48
BLOCK = 4
DIRECTIONS = [(1, 0), (-1, 0), (0, 1), (0, -1), (1, 1), (1, -1), (-1, 1), (-1, -1)]


def gll_weights():
    return np.array(
        [
            1.0 / 28.0,
            0.2107042271435061,
            0.3411226924835044,
            0.4124587946587038,
            0.4124587946587038,
            0.3411226924835044,
            0.2107042271435061,
            1.0 / 28.0,
        ]
    )


def gll_derivative():
    points = np.array(
        [
            -1.0,
            -0.8717401485096066,
            -0.5917001814331423,
            -0.2092992179024789,
            0.2092992179024789,
            0.5917001814331423,
            0.8717401485096066,
            1.0,
        ]
    )
    identity = np.eye(8) > 0
    spacing = np.where(identity, 1.0, points[:, None] - points[None, :])
    barycentric = 1.0 / np.prod(spacing, axis=1)
    matrix = np.where(identity, 0.0, barycentric[None, :] / barycentric[:, None] / spacing)
    return np.where(identity, -np.sum(matrix, axis=1)[:, None], matrix)


WEIGHTS = gll_weights()
STIFF = gll_derivative().T @ np.diag(WEIGHTS) @ gll_derivative()


def split(matrix):
    high = matrix.astype(ml_dtypes.bfloat16)
    low = (matrix - high.astype(np.float64)).astype(ml_dtypes.bfloat16)
    return high, low


def band(cells, size):
    first, second = np.zeros((size, size)), np.zeros((size, size))
    for e in range(cells):
        for b in range(7):
            first[7 * e + b, 7 * e : 7 * e + 8] = STIFF[b]
        second[7 * e + 7, 7 * e : 7 * e + 8] = STIFF[7]
    return first, second


def tables(cap_x, cap_y, layers):
    first, second = band(layers, LANES)
    high, low = split(np.concatenate([first, second], axis=0).T)
    vertical = np.concatenate([high, high, low], axis=0)
    first, second = band(cap_y, ROWS)
    stacked = np.concatenate([np.kron(np.eye(4), first), np.kron(np.eye(4), second)], axis=0)
    high, low = split(stacked)
    across = np.concatenate([high, high, low], axis=1)
    depth = np.zeros((LANES, 3 * LANES))
    for h in range(layers):
        depth[h, 7 * h : 7 * h + 8] = WEIGHTS
        depth[h, LANES + 7 * h : LANES + 7 * h + 7] = 1.0
        depth[h, 2 * LANES + 7 * h + 7] = 1.0
    weigh, pick, ends = np.zeros((ROWS, 8)), np.zeros((ROWS, 8)), np.zeros((ROWS, 8))
    for f in range(cap_y):
        weigh[7 * f : 7 * f + 8, f] = WEIGHTS
        pick[7 * f : 7 * f + 7, f] = 1.0
        ends[7 * f + 7, f] = 1.0
    unit = np.eye(cap_x)
    widen = np.concatenate([np.kron(unit, weigh), np.kron(unit, pick), np.kron(unit, ends)], axis=0)
    widen = np.pad(widen, ((0, 0), (0, LANES - widen.shape[1])))
    factor = np.zeros((ROWS + 8, LANES))
    factor[: 7 * cap_y] = STIFF[np.arange(7 * cap_y) % 7, np.arange(7 * cap_y) % 7][:, None]
    factor[ROWS:, : 7 * layers] = STIFF[np.arange(7 * layers) % 7, np.arange(7 * layers) % 7][None, :]
    return (
        vertical,
        across,
        depth.astype(np.float32),
        widen.astype(np.float32),
        factor.astype(np.float32),
    )


def plane(x):
    return pl.ds(pl.multiple_of(x * ROWS, ROWS), ROWS)


def total(values):
    return jnp.sum(values, axis=(0, 1), keepdims=True)


def iota(shape, dim):
    return lax.broadcasted_iota(jnp.int32, shape, dim)


def pieces(values):
    first = values.astype(jnp.bfloat16)
    rest = values - first.astype(jnp.float32)
    second = rest.astype(jnp.bfloat16)
    third = (rest - second.astype(jnp.float32)).astype(jnp.bfloat16)
    return [first, second, third]


def exact_dot(values, chosen):
    rows = values.shape[0]
    result = jnp.dot(
        jnp.concatenate(pieces(values), axis=0), chosen, preferred_element_type=jnp.float32
    )
    return result[0:rows] + result[rows : 2 * rows] + result[2 * rows : 3 * rows]


def kernel(
    nx, ny, cap_x, cap_y, layers, bx, by,
    wx_ref, wy_ref, load_any, diff_any, kappa_any, factor_any,
    vertical_any, across_any, depth_any, widen_any, coefficient_any,
    solution_ref, residual_ref,
    load_ref, diff_ref, kappa_ref,
    vertical_ref, across_ref, depth_ref, widen_ref, coefficient_ref,
    f_z, f_im, f_w, f_d, f_r, f_sol, f_inv, f_share, f_mass, f_ya, f_yb, f_za, f_zb,
    e_px, e_big, e_ya, e_yb, squares, sq_kappa,
    rows_x, gather_map, spread_map,
    halo_sx, halo_sy, halo_sc, halo_rx, halo_ry, halo_rc,
    grid_s, grid_r, chunk_s, chunk_r, back_s, back_r, last_s, last_r, end_s, end_r,
    in_sem, own_sem, x_send, x_recv, ring_send, ring_recv,
    h_send, h_recv, r_send, r_recv, l_send, l_recv,
):
    p, q = lax.axis_index("gx"), lax.axis_index("gy")
    wx, wy = wx_ref[0], wy_ref[0]
    groups = chunk_s.shape[1] - 1
    width = groups * LANES
    end_x, end_y = 7 * wx, 7 * wy
    near, far = bx * by, (nx // bx) * (ny // by)
    ax, ay = nx // bx, ny // by
    bi, bj, ai, aj = lax.rem(p, bx), lax.rem(q, by), p // bx, q // by
    mine, block_id = bi * by + bj, ai * ay + aj

    def beside(dx, dy):
        return (lax.rem(p + dx + nx, nx), lax.rem(q + dy + ny, ny))

    def in_block(index):
        return (ai * bx + index // by, aj * by + lax.rem(index, by))

    def across(index):
        return (index // ay * bx + bi, lax.rem(index, ay) * by + bj)

    barrier = pltpu.get_barrier_semaphore()

    def greet(device):
        pl.semaphore_signal(barrier, inc=1, device_id=device, device_id_type=MESH)

    def greet_near(o, _):
        greet(in_block(lax.rem(mine + o, near)))
        return 0

    def greet_far(o, _):
        greet(across(lax.rem(block_id + o, far)))
        return 0

    lax.fori_loop(1, near, greet_near, 0)
    lax.fori_loop(1, far, greet_far, 0)
    for dx, dy in DIRECTIONS:
        greet(beside(dx, dy))

    arrivals = []
    for i, (source, target) in enumerate((
        (diff_any, diff_ref), (kappa_any, kappa_ref), (depth_any, depth_ref),
        (widen_any, widen_ref), (coefficient_any, coefficient_ref), (load_any, load_ref),
        (vertical_any, vertical_ref), (across_any, across_ref),
    )):
        copy = pltpu.make_async_copy(source, target, in_sem.at[i])
        copy.start()
        arrivals.append(copy)

    def remote(source, target, send, recv, device):
        return pltpu.make_async_remote_copy(
            src_ref=source,
            dst_ref=target,
            send_sem=send,
            recv_sem=recv,
            device_id=device,
            device_id_type=MESH,
        )

    def columns(index):
        return pl.ds(pl.multiple_of(index * width, LANES), width)

    def rows_of(j):
        return pl.ds(pl.multiple_of((j + 1) * 16, 16), 16)

    own_rows = pltpu.make_async_copy(
        factor_any.at[:, columns(mine)], rows_x.at[bi + 1, rows_of(bj), :], own_sem.at[0]
    )
    own_rows.start()

    def flag(condition):
        return jnp.where(condition, 1.0, 0.0).astype(jnp.float32)

    has_left, has_right = flag(p > 0), flag(p < nx - 1)
    has_below, has_above = flag(q > 0), flag(q < ny - 1)

    pl.semaphore_wait(barrier, near + far - 2 + len(DIRECTIONS))

    def scatter_copy(o):
        peer = lax.rem(mine + o, near)
        return remote(
            factor_any.at[:, columns(peer)],
            rows_x.at[bi + 1, rows_of(bj), :],
            x_send.at[o],
            x_recv.at[o],
            in_block(peer),
        )

    def scatter(o, _):
        scatter_copy(o).start()
        return 0

    lax.fori_loop(1, near, scatter, 0)

    squares[...] = jnp.zeros_like(squares)
    sq_kappa[...] = jnp.zeros_like(sq_kappa)
    for copy in arrivals[0:5]:
        copy.wait()
    inside = iota((cap_y, layers), 0) < wy
    for e in range(cap_x):
        keep = inside & (e < wx)
        squares[8 * e : 8 * e + cap_y, 0:layers] = jnp.where(keep, diff_ref[e], 0.0)
        sq_kappa[8 * e : 8 * e + cap_y, 0:layers] = jnp.where(keep, kappa_ref[e], 0.0)
    deep = jnp.dot(squares[...], depth_ref[...], precision=HIGHEST, preferred_element_type=jnp.float32)
    deep_kappa = jnp.dot(
        sq_kappa[...], depth_ref[:, 0:LANES], precision=HIGHEST, preferred_element_type=jnp.float32
    )
    tall = cap_x * ROWS
    big = jnp.dot(
        widen_ref[0:tall, :],
        jnp.concatenate([deep, deep_kappa], axis=1),
        precision=HIGHEST,
        preferred_element_type=jnp.float32,
    )
    both = jnp.dot(
        widen_ref[tall : 3 * tall, :],
        deep[:, 0:LANES],
        precision=HIGHEST,
        preferred_element_type=jnp.float32,
    )
    zero_plane = jnp.zeros((ROWS, LANES), jnp.float32)
    for ref in (e_px, e_ya, e_yb):
        ref[0:ROWS, :] = zero_plane
        ref[tall + ROWS : tall + 2 * ROWS, :] = zero_plane
    for place in (0, tall + ROWS):
        e_big[place : place + ROWS, :] = jnp.zeros((ROWS, 3 * LANES), jnp.float32)
    e_px[ROWS : ROWS + tall, :] = big[:, 0:LANES]
    e_big[ROWS : ROWS + tall, :] = big[:, LANES : 4 * LANES]
    e_ya[ROWS : ROWS + tall, :] = both[0:tall]
    e_yb[ROWS : ROWS + tall, :] = both[tall : 2 * tall]

    fields = (f_z, f_im, f_r, f_inv, f_mass, f_ya, f_yb, f_za, f_zb)
    for ref in fields:
        for x in range(7 * cap_x, PLANES):
            ref[x * ROWS : (x + 1) * ROWS, :] = zero_plane

    sources = (
        (f_za, e_big, 0), (f_zb, e_big, 1), (f_mass, e_big, 2), (f_ya, e_ya, 0), (f_yb, e_yb, 0),
    )
    row_factor = coefficient_ref[0:ROWS, :]
    depth_factor = coefficient_ref[ROWS : ROWS + 1, :]
    corner = float(STIFF[7, 7])

    def fill_plane(x, e, b):
        values = []
        for target, source, lane in sources:
            lanes = slice(lane * LANES, (lane + 1) * LANES)
            value = float(WEIGHTS[b]) * source[plane(e + 1), lanes]
            if b == 0:
                value = value + float(WEIGHTS[7]) * source[plane(e), lanes]
            target[plane(x), :] = value
            values.append(value)
        za, zb, mass, ya, yb = values
        diagonal = mass + ya * row_factor + yb * corner + za * depth_factor + zb * corner
        diagonal = diagonal + float(STIFF[b, b]) * e_px[plane(e + 1), :]
        if b == 0:
            diagonal = diagonal + float(STIFF[7, 7]) * e_px[plane(e), :]
        f_inv[plane(x), :] = diagonal

    def fill(e, _):
        for b in range(7):
            fill_plane(7 * e + b, e, b)
        return 0

    lax.fori_loop(0, cap_x, fill, 0)
    fill_plane(7 * cap_x, cap_x, 0)

    slots_x, slots_y = load_ref.shape[0], load_ref.shape[1]
    row = iota((slots_y, LANES), 0)
    real = iota((slots_y, LANES), 1) <= 7 * layers
    f_r[...] = jnp.zeros_like(f_r)
    arrivals[5].wait()

    def take(x, _):
        value = jnp.where(x < end_x, load_ref[x], jnp.where(x == end_x, load_ref[slots_x - 1], 0.0))
        last = value[slots_y - 1 : slots_y, :]
        value = jnp.where(row < end_y, value, jnp.where(row == end_y, last, 0.0))
        f_r[pl.ds(pl.multiple_of(x * ROWS, ROWS), slots_y), :] = jnp.where(real, value, 0.0)
        return 0

    lax.fori_loop(0, slots_x, take, 0)

    def high_plane(ref):
        value = jnp.zeros((ROWS, LANES), jnp.float32)
        for j in range(1, cap_x + 1):
            value = value + jnp.where(wx == j, ref[7 * j * ROWS : (7 * j + 1) * ROWS, :], 0.0)
        return value

    def side(j):
        return pl.ds(7 * j, PLANES, stride=ROWS)

    def high_row(plane_value):
        value = jnp.zeros((1, LANES), jnp.float32)
        for j in range(1, cap_y + 1):
            value = value + jnp.where(wy == j, plane_value[7 * j : 7 * j + 1, :], 0.0)
        return value

    def halo_copies(h):
        copies = []
        for k, (dx, dy) in enumerate(DIRECTIONS):
            if dy == 0:
                slot = (h, 0 if dx > 0 else 1)
                source, target = halo_sx.at[slot], halo_rx.at[slot]
            elif dx == 0:
                slot = (h, 0 if dy > 0 else 1)
                source, target = halo_sy.at[slot], halo_ry.at[slot]
            else:
                source, target = halo_sc.at[h, k - 4], halo_rc.at[h, k - 4]
            copies.append(remote(source, target, h_send.at[h, k], h_recv.at[h, k], beside(dx, dy)))
        return copies

    def halo_start(h, ref):
        low, high = ref[0:ROWS, :], high_plane(ref)
        halo_sx[h, 0] = high
        halo_sx[h, 1] = low
        above = jnp.zeros((PLANES, LANES), jnp.float32)
        for j in range(1, cap_y + 1):
            above = above + jnp.where(wy == j, ref[side(j), :], 0.0)
        halo_sy[h, 0] = above
        halo_sy[h, 1] = ref[side(0), :]
        rows = (high_row(high), high[0:1, :], high_row(low), low[0:1, :])
        for k, value in enumerate(rows):
            halo_sc[h, k] = jnp.broadcast_to(value, (8, LANES))
        copies = halo_copies(h)
        for copy in copies:
            copy.start()
        return copies

    place = iota((PLANES, LANES), 0)

    def halo_finish(h, ref, copies):
        for copy in copies:
            copy.wait()
        ref[0:ROWS, :] = ref[0:ROWS, :] + has_left * halo_rx[h, 0]
        from_right = has_right * halo_rx[h, 1]
        for j in range(1, cap_x + 1):
            rows = slice(7 * j * ROWS, (7 * j + 1) * ROWS)
            ref[rows, :] = ref[rows, :] + jnp.where(wx == j, from_right, 0.0)

        def line(side_value, first, second):
            side_value = side_value + jnp.where(place == 0, has_left * first[0:1, :], 0.0)
            return side_value + jnp.where(place == end_x, has_right * second[0:1, :], 0.0)

        below = has_below * line(halo_ry[h, 0], halo_rc[h, 0], halo_rc[h, 2])
        above = has_above * line(halo_ry[h, 1], halo_rc[h, 1], halo_rc[h, 3])
        ref[side(0), :] = ref[side(0), :] + below
        for j in range(1, cap_y + 1):
            ref[side(j), :] = ref[side(j), :] + jnp.where(wy == j, above, 0.0)

    deep_node, deep_lane = iota((LANES, LANES), 0), iota((LANES, LANES), 1)
    for dy in (-1, 0, 1):
        part = slice((dy + 1) * LANES, (dy + 2) * LANES)
        start = (bj + 1 + dy) * 16
        gather_map[part, :] = flag(deep_lane == start + deep_node // 8).astype(jnp.bfloat16)
        spread_map[:, part] = flag(deep_node == start + deep_lane // 8).astype(jnp.bfloat16)
    grid_row = iota((8, LANES), 0)
    row32 = iota((ROWS, LANES), 0)
    chunk = 4 * ROWS
    chunks = (7 * cap_x + 4) // 4

    def coarse_sums(ref):
        def add(i, value):
            return value + jnp.sum(
                ref[pl.ds(pl.multiple_of(i * chunk, chunk), chunk), :].reshape(4, ROWS, LANES), axis=0
            )

        middle = lax.fori_loop(0, chunks, add, zero_plane)
        low, high = 0.5 * has_left * ref[0:ROWS, :], 0.5 * has_right * high_plane(ref)
        sums = [jnp.zeros((8, LANES), jnp.float32)] * 3
        for dx, value in ((-1, low), (0, middle - low - high), (1, high)):
            below = 0.5 * has_below * value[0:1, :]
            above = 0.5 * has_above * high_row(value)
            centre = jnp.sum(value, axis=0, keepdims=True) - below - above
            for k, profile in enumerate((below, centre, above)):
                sums[k] = sums[k] + jnp.where(grid_row == bi + 1 + dx, profile, 0.0)
        return exact_dot(jnp.concatenate(sums, axis=1), gather_map[...])

    def wait_in(buffer, count, send, recv):
        part = buffer.at[pl.ds(0, count)]
        remote(part, part, send, recv, beside(1, 0)).wait_recv()

    def wait_out(buffer, count, send, recv):
        part = buffer.at[pl.ds(0, count)]
        remote(part, part, send, recv, beside(1, 0)).wait_send()

    def exchange_start(source, target, count, me, device, send, recv):
        def go(o, _):
            remote(source, target.at[me], send, recv, device(lax.rem(me + o, count))).start()
            return 0

        lax.fori_loop(1, count, go, 0)
        target[me] = source[...]

    def reduce_start(a, ref):
        grid_s[a] = coarse_sums(ref)
        exchange_start(
            grid_s.at[a], grid_r.at[a], near, mine, in_block, r_send.at[a, 0], r_recv.at[a, 0]
        )

    lane = iota((1, LANES), 1)

    def scalar_row(values):
        result = jnp.zeros((1, LANES), jnp.float32)
        for i, value in enumerate(values):
            result = jnp.where(lane == i, value, result)
        return result

    def pick(values, i):
        return total(jnp.where(lane == i, values, 0.0))

    grid_rows, grid_lanes = bx + 2, (by + 2) * 16

    def reduce_middle(a, scalars):
        wait_in(grid_r.at[a], near - 1, r_send.at[a, 0], r_recv.at[a, 0])
        turned = jnp.sum(grid_r[a], axis=0).T
        value = jnp.zeros((8, width), jnp.float32)
        for i in range(grid_rows):
            product = rows_x[i] * turned[0:grid_lanes, i : i + 1]
            value = value + jnp.sum(product.reshape(grid_lanes // 8, 8, width), axis=0)
        value = jnp.sum(value, axis=0, keepdims=True)
        for g in range(groups):
            chunk_s[a, g : g + 1, :] = value[:, g * LANES : (g + 1) * LANES]
        chunk_s[a, groups : groups + 1, :] = scalar_row(scalars)
        exchange_start(
            chunk_s.at[a], chunk_r.at[a], far, block_id, across, r_send.at[a, 1], r_recv.at[a, 1]
        )

    def reduce_finish(a, extra):
        wait_in(chunk_r.at[a], far - 1, r_send.at[a, 1], r_recv.at[a, 1])
        sums = jnp.sum(chunk_r[a], axis=0)
        through = sums[0:groups, :]
        turned = jnp.zeros((grid_lanes, LANES), jnp.float32)
        wide_lane = iota((grid_lanes, LANES), 1)
        for i in range(grid_rows):
            product = rows_x[i, :, 0:LANES] * through[0:1, :]
            for g in range(1, groups):
                product = product + rows_x[i, :, g * LANES : (g + 1) * LANES] * through[g : g + 1, :]
            turned = jnp.where(wide_lane == i, jnp.sum(product, axis=1, keepdims=True), turned)
        turned = jnp.concatenate(
            [turned, jnp.zeros((LANES - grid_lanes, LANES), jnp.float32)], axis=0
        )
        scalars = sums[groups : groups + 1, :]
        if extra is not None:
            scalars = jnp.where(lane == 8, extra, scalars)
        back_s[a] = jnp.where(grid_row == 7, scalars, turned.T[0:8, :])
        exchange_start(
            back_s.at[a], back_r.at[a], near, mine, in_block, r_send.at[a, 2], r_recv.at[a, 2]
        )
        wait_in(back_r.at[a], near - 1, r_send.at[a, 2], r_recv.at[a, 2])
        grid = jnp.sum(back_r[a], axis=0)
        wait_out(grid_r.at[a], near - 1, r_send.at[a, 0], r_recv.at[a, 0])
        wait_out(chunk_r.at[a], far - 1, r_send.at[a, 1], r_recv.at[a, 1])
        wait_out(back_r.at[a], near - 1, r_send.at[a, 2], r_recv.at[a, 2])
        return grid, grid[7:8, :], through

    def coarse_planes(grid):
        deep_values = exact_dot(grid, spread_map[...])

        def spread(dx):
            line = jnp.sum(jnp.where(iota((8, 3 * LANES), 0) == bi + 1 + dx, deep_values, 0.0), axis=0, keepdims=True)
            below, centre, above = (line[:, k * LANES : (k + 1) * LANES] for k in range(3))
            value = jnp.where(row32 == 0, centre + 0.5 * has_below * (below - centre), centre)
            return jnp.where(row32 == end_y, value + 0.5 * has_above * (above - centre), value)

        middle = spread(0)
        first = middle + 0.5 * has_left * (spread(-1) - middle)
        second = middle + 0.5 * has_right * (spread(1) - middle)
        return first, middle, second

    def coarse_at(x, planes):
        first, middle, second = planes
        return jnp.where(x == 0, first, jnp.where(x == end_x, second, middle))

    def apply_operator():
        def along_x(e, carried):
            values = [f_z[plane(7 * e + c), :] for c in range(8)]
            sums = [values[c] + values[7 - c] for c in range(4)]
            gaps = [values[c] - values[7 - c] for c in range(4)]
            scale = e_px[plane(e + 1), :]
            results = [None] * 8
            for b in range(4):
                even = sum(float(0.5 * (STIFF[b, c] + STIFF[b, 7 - c])) * sums[c] for c in range(4))
                odd = sum(float(0.5 * (STIFF[b, c] - STIFF[b, 7 - c])) * gaps[c] for c in range(4))
                results[b] = scale * (even + odd)
                results[7 - b] = scale * (even - odd)
            f_im[plane(7 * e), :] = carried + results[0]
            for b in range(1, 7):
                f_im[plane(7 * e + b), :] = results[b]
            return results[7]

        carried = lax.fori_loop(0, cap_x, along_x, zero_plane)
        f_im[plane(7 * cap_x), :] = carried

        def along_rest(i, product):
            rows = pl.ds(pl.multiple_of(i * chunk, chunk), chunk)
            value = f_z[rows, :]
            high = value.astype(jnp.bfloat16)
            low = (value - high.astype(jnp.float32)).astype(jnp.bfloat16)
            deep = jnp.dot(
                jnp.concatenate([high, low, high], axis=1),
                vertical_ref[...],
                preferred_element_type=jnp.float32,
            )
            wide = jnp.dot(
                across_ref[...],
                jnp.concatenate([high, low, high], axis=0),
                preferred_element_type=jnp.float32,
            )
            image = f_im[rows, :] + f_mass[rows, :] * value
            image = image + f_ya[rows, :] * wide[0:chunk] + f_yb[rows, :] * wide[chunk:]
            image = image + f_za[rows, :] * deep[:, 0:LANES] + f_zb[rows, :] * deep[:, LANES:]
            f_im[rows, :] = image
            return product + jnp.sum((value * image).reshape(chunk // 8, 8, LANES), axis=0)

        product = lax.fori_loop(0, chunks, along_rest, jnp.zeros((8, LANES), jnp.float32))
        return total(product)

    reduce_start(0, f_r)
    load_copies = halo_start(0, f_r)
    diagonal_copies = halo_start(1, f_inv)

    own_rows.wait()

    def scatter_wait(o, _):
        scatter_copy(o).wait()
        return 0

    lax.fori_loop(1, near, scatter_wait, 0)
    spans = {1: (slice(bx, bx + 1), slice(0, 1)), -1: (slice(1, 2), slice(bx + 1, bx + 2))}
    spans[0] = (slice(1, bx + 1), slice(1, bx + 1))
    across_spans = {1: (by, 0, 1), -1: (1, by + 1, 1), 0: (1, 1, by)}
    ring = []
    for k, (dx, dy) in enumerate(DIRECTIONS):
        (source_x, target_x), (source_y, target_y, count) = spans[dx], across_spans[dy]
        copy = remote(
            rows_x.at[source_x, pl.ds(source_y * 16, count * 16), :],
            rows_x.at[target_x, pl.ds(target_y * 16, count * 16), :],
            ring_send.at[k],
            ring_recv.at[k],
            beside(dx * bx, dy * by),
        )
        copy.start()
        ring.append(copy)

    halo_finish(0, f_r, load_copies)
    halo_finish(1, f_inv, diagonal_copies)
    share_low = jnp.where(row32 == 0, 1.0 - 0.5 * has_below, 1.0)
    share_row = jnp.where(row32 == end_y, 1.0 - 0.5 * has_above, share_low)

    def share_x(x):
        low = jnp.where(x == 0, 1.0 - 0.5 * has_left, 1.0)
        return jnp.where(x == end_x, 1.0 - 0.5 * has_right, low)

    def invert(x, value):
        diagonal = f_inv[plane(x), :]
        inverse = jnp.where(diagonal > 0.0, 1.0 / jnp.where(diagonal > 0.0, diagonal, 1.0), 0.0)
        f_inv[plane(x), :] = inverse
        share = jnp.where(diagonal > 0.0, share_row * share_x(x), 0.0)
        f_share[plane(x), :] = share
        resid = f_r[plane(x), :]
        f_sol[plane(x), :] = zero_plane
        f_w[plane(x), :] = zero_plane
        f_d[plane(x), :] = zero_plane
        return value + share * inverse * resid * resid

    planes = 7 * cap_x + 1
    jacobi = total(lax.fori_loop(0, planes, invert, zero_plane))
    for copy in ring:
        copy.wait()
    for copy in arrivals[6:]:
        copy.wait()
    reduce_middle(0, [])
    grid, _, through = reduce_finish(0, None)
    coarse = coarse_planes(grid)

    def begin(x, _):
        inverse = f_inv[plane(x), :]
        value = jnp.where(inverse > 0.0, coarse_at(x, coarse), 0.0)
        f_z[plane(x), :] = inverse * f_r[plane(x), :] + value
        return 0

    lax.fori_loop(0, planes, begin, 0)

    cross = jnp.zeros((1, 1), jnp.float32)
    beta, rho, curvature = cross, None, cross
    through_w, grid_w = jnp.zeros_like(through), jnp.zeros_like(grid)

    def scalars_of(values, squared):
        rho_now = pick(values, 2) + squared
        beta_now = jnp.zeros((1, 1), jnp.float32) if rho is None else rho_now / rho
        bent = pick(values, 0) + 2.0 * beta_now * pick(values, 1) + beta_now * beta_now * curvature
        return rho_now, beta_now, bent

    for i in range(ITERS):
        own = apply_operator()
        squared = total(through * through)
        if i + 1 < ITERS:
            reduce_start(i + 1, f_im)
            image_copies = halo_start(2 + i, f_im)
            reduce_middle(i + 1, [own, cross, jacobi])
            halo_finish(2 + i, f_im, image_copies)
            grid_q, values, through_q = reduce_finish(i + 1, squared)
            rho, beta, curvature = scalars_of(values, pick(values, 8))
            step = rho / curvature
            grid_w = grid_q + beta * grid_w
            through_w = through_q + beta * through_w
            grid = grid - step * grid_w
            through = through - step * through_w
            coarse = coarse_planes(grid)

            def advance(x, sums):
                here = plane(x)
                old = f_z[here, :]
                direction = old + beta * f_d[here, :]
                image = f_im[here, :] + beta * f_w[here, :]
                f_d[here, :] = direction
                f_w[here, :] = image
                f_sol[here, :] = f_sol[here, :] + step * direction
                resid = f_r[here, :] - step * image
                f_r[here, :] = resid
                scaled = f_inv[here, :] * resid
                share = f_share[here, :]
                value = scaled + jnp.where(share > 0.0, coarse_at(x, coarse), 0.0)
                f_z[here, :] = value
                return sums[0] + share * scaled * resid, sums[1] + share * value * image

            jacobi, cross = lax.fori_loop(0, planes, advance, (zero_plane, zero_plane))
            jacobi, cross = total(jacobi), total(cross)
        else:
            last_s[...] = scalar_row([own, cross, jacobi])
            exchange_start(last_s, last_r, far, block_id, across, l_send.at[0], l_recv.at[0])
            image_copies = halo_start(2 + i, f_im)
            halo_finish(2 + i, f_im, image_copies)
            wait_in(last_r, far - 1, l_send.at[0], l_recv.at[0])
            end_s[...] = jnp.where(lane == 8, squared, jnp.sum(last_r[...], axis=0))
            exchange_start(end_s, end_r, near, mine, in_block, l_send.at[1], l_recv.at[1])
            wait_in(end_r, near - 1, l_send.at[1], l_recv.at[1])
            values = jnp.sum(end_r[...], axis=0)
            rho, beta, curvature = scalars_of(values, pick(values, 8))
            step = rho / curvature
            wait_out(last_r, far - 1, l_send.at[0], l_recv.at[0])
            wait_out(end_r, near - 1, l_send.at[1], l_recv.at[1])

    def put(target, x, value):
        last = high_row(value)
        rows = value[0:slots_y, :]
        rows = jnp.where(row < end_y, rows, jnp.where(row == slots_y - 1, last, 0.0))
        target[x] = rows

    def finish(x, _):
        here = plane(x)
        found = f_sol[here, :] + step * (f_z[here, :] + beta * f_d[here, :])
        resid = f_r[here, :] - step * (f_im[here, :] + beta * f_w[here, :])
        f_sol[here, :] = found
        f_r[here, :] = resid
        put(solution_ref, x, jnp.where(x < end_x, found, 0.0))
        put(residual_ref, x, jnp.where(x < end_x, resid, 0.0))
        return 0

    lax.fori_loop(0, planes, finish, 0)
    put(solution_ref, slots_x - 1, high_plane(f_sol))
    put(residual_ref, slots_x - 1, high_plane(f_r))


def body(nx, ny, right_side, diffusion, kappa, widths_x, widths_y, factor):
    cap_x, cap_y, layers = diffusion.shape
    bx, by = BLOCK, BLOCK
    near, far = bx * by, (nx // bx) * (ny // by)
    groups = factor.shape[1] // (near * LANES)
    f32, bf16 = jnp.float32, jnp.bfloat16
    smem = pl.BlockSpec(memory_space=pltpu.SMEM)
    vmem = pl.BlockSpec(memory_space=pltpu.VMEM)
    hbm = pl.BlockSpec(memory_space=pltpu.HBM)
    tall = cap_x * ROWS
    dma = pltpu.SemaphoreType.DMA
    constants = [jnp.asarray(table) for table in tables(cap_x, cap_y, layers)]

    def room(*shape, dtype=f32):
        return pltpu.VMEM(shape, dtype)

    scratch = [room(*array.shape, dtype=array.dtype) for array in (right_side, diffusion, kappa)]
    scratch += [room(*array.shape, dtype=array.dtype) for array in constants]
    scratch += [room(PLANES * ROWS, LANES)] * 13
    scratch += [
        room(tall + 2 * ROWS, LANES),
        room(tall + 2 * ROWS, 3 * LANES),
        room(tall + 2 * ROWS, LANES),
        room(tall + 2 * ROWS, LANES),
        room(LANES, LANES),
        room(LANES, LANES),
        room(bx + 2, (by + 2) * 16, groups * LANES),
        room(3 * LANES, LANES, dtype=bf16),
        room(LANES, 3 * LANES, dtype=bf16),
    ]
    halos = 2 + ITERS
    for _ in range(2):
        scratch += [
            room(halos, 2, ROWS, LANES),
            room(halos, 2, PLANES, LANES),
            room(halos, 4, 8, LANES),
        ]
    scratch += [
        room(ITERS, 8, LANES),
        room(ITERS, near, 8, LANES),
        room(ITERS, groups + 1, LANES),
        room(ITERS, far, groups + 1, LANES),
        room(ITERS, 8, LANES),
        room(ITERS, near, 8, LANES),
        room(1, LANES),
        room(far, 1, LANES),
        room(1, LANES),
        room(near, 1, LANES),
        dma((8,)), dma((1,)), dma((near,)), dma((near,)), dma((8,)), dma((8,)),
        dma((halos, 8)), dma((halos, 8)), dma((ITERS, 3)), dma((ITERS, 3)), dma((2,)), dma((2,)),
    ]
    shape = jax.ShapeDtypeStruct(right_side.shape, f32)
    return pl.pallas_call(
        functools.partial(kernel, nx, ny, cap_x, cap_y, layers, bx, by),
        out_shape=(shape, shape),
        in_specs=[smem, smem] + [hbm] * 9,
        out_specs=(vmem, vmem),
        scratch_shapes=scratch,
        compiler_params=pltpu.CompilerParams(
            collective_id=0, has_side_effects=True, vmem_limit_bytes=48 * 1024 * 1024
        ),
    )(widths_x, widths_y, right_side, diffusion, kappa, factor, *constants)


def solution(mesh):
    nx, ny = mesh.shape["gx"], mesh.shape["gy"]
    in_specs = (
        P("gx", "gy", None),
        P("gx", "gy", None),
        P("gx", "gy", None),
        P("gx"),
        P("gy"),
        P(("gx", "gy"), None),
    )
    out_specs = (P("gx", "gy", None), P("gx", "gy", None))
    return jax.shard_map(
        functools.partial(body, nx, ny),
        mesh=mesh,
        in_specs=in_specs,
        out_specs=out_specs,
        check_vma=False,
    )
```

time: 131 us -> 123 us (0.939)
  Pallas kernels: 119 us -> 111 us
    pallas_call x1, Pallas kernels: 119 us -> 111 us  [body(): pl.pallas_call(functools.partial(kernel, nx, ny, cap_x, cap_y, layers, bx...]
where the time goes in v2:
time: 123 us; the launch traced here: 122 us
  Pallas kernels  111 us (90%)
  local copies, waits for them, and re-layouts  9.73 us (8%)
  between operations  1.95 us (2%)
    pallas_call x1, Pallas kernels, body(): pl.pallas_call(functools.partial(kernel, nx, ny, cap_x, cap_y, layers, bx...  111 us
    unnamed x20, local copies, waits for them, and re-layouts  9.73 us

profile of v2, /device:TPU:1, one launch (start us, length us, event | category | flops | bytes accessed | tf_op | source)
XLA Modules:
  0.0 122.3 jit_solution(14753947003315359041)
XLA Ops:
  1.9 0.0 copy-start
  1.9 1.1 copy-done
  3.0 0.0 copy-start.1
  3.0 1.0 copy-done.1
  4.1 0.0 copy-start.2
  4.1 1.0 copy-done.2
  5.0 0.0 copy-start.3
  5.0 0.9 copy-done.3
  6.0 0.0 copy-start.4
  6.0 0.9 copy-done.4
  6.9 0.0 copy-start.5
  6.9 0.9 copy-done.5
  7.8 0.0 copy-start.6
  7.8 0.7 copy-done.6
  8.5 0.0 copy-start.7
  8.5 0.7 copy-done.7
  9.2 0.0 copy-start.8
  9.3 0.7 copy-done.8
  10.0 110.6 %shard_map.122 = (f32[43,29,128]{2,1,0:T(8,128)S(1)}, f32[43,29,128]{2,1,0:T(8,128)S(1)}) custom-call(s32[1]{0:T(128)S(6)} %copy.15.wx_ref, s32[1]{0:T(128)S(6)} %copy.16.wy_ref, f32[43,29,128]{2,1,0:T(8,128)S(1)} %copy-done, f32[6,4,18]{2,1,0:T(4,128)S(1)} %copy-done.7, f32[6,4,18]{2,1,0:T(4,128)S(1)} %copy-done.8, f32[16,8192]{1,0:T(8,128)S(1)} %copy-done.1, ...), custom_call_target="tpu_custom_call" | custom-call | tf_op jit(solution)/shard_map/pallas_call | solution.py:766
  120.6 0.9 copy.17
  121.4 0.9 copy.18
Async XLA Ops:
  1.9 1.1 copy-start
  3.0 1.0 copy-start.1
  4.1 1.0 copy-start.2
  5.0 0.9 copy-start.3
  6.0 0.9 copy-start.4
  6.9 0.9 copy-start.5
  7.8 0.7 copy-start.6
  8.5 0.7 copy-start.7
  9.2 0.7 copy-start.8

commit v3 on v2

--- a/solution.py
+++ b/solution.py
@@ -75,12 +75,10 @@
 
 def tables(cap_x, cap_y, layers):
     first, second = band(layers, LANES)
-    high, low = split(np.concatenate([first, second], axis=0).T)
-    vertical = np.concatenate([high, high, low], axis=0)
+    vertical = split(np.concatenate([first, second], axis=0).T)
     first, second = band(cap_y, ROWS)
     stacked = np.concatenate([np.kron(np.eye(4), first), np.kron(np.eye(4), second)], axis=0)
-    high, low = split(stacked)
-    across = np.concatenate([high, high, low], axis=1)
+    across = split(stacked)
     depth = np.zeros((LANES, 3 * LANES))
     for h in range(layers):
         depth[h, 7 * h : 7 * h + 8] = WEIGHTS
@@ -97,13 +95,10 @@
     factor = np.zeros((ROWS + 8, LANES))
     factor[: 7 * cap_y] = STIFF[np.arange(7 * cap_y) % 7, np.arange(7 * cap_y) % 7][:, None]
     factor[ROWS:, : 7 * layers] = STIFF[np.arange(7 * layers) % 7, np.arange(7 * layers) % 7][None, :]
-    return (
-        vertical,
-        across,
-        depth.astype(np.float32),
-        widen.astype(np.float32),
-        factor.astype(np.float32),
-    )
+    parts = [half for part in vertical for half in (part[:, :LANES], part[:, LANES:])]
+    parts += [*across]
+    parts += [depth[:, k * LANES : (k + 1) * LANES] for k in range(3)] + [widen, factor]
+    return np.concatenate([part.astype(np.float32) for part in parts], axis=0)
 
 
 def plane(x):
@@ -137,10 +132,9 @@
 def kernel(
     nx, ny, cap_x, cap_y, layers, bx, by,
     wx_ref, wy_ref, load_any, diff_any, kappa_any, factor_any,
-    vertical_any, across_any, depth_any, widen_any, coefficient_any,
+    table_any,
     solution_ref, residual_ref,
-    load_ref, diff_ref, kappa_ref,
-    vertical_ref, across_ref, depth_ref, widen_ref, coefficient_ref,
+    load_ref, diff_ref, kappa_ref, table_ref, vertical_ref, across_ref,
     f_z, f_im, f_w, f_d, f_r, f_sol, f_inv, f_share, f_mass, f_ya, f_yb, f_za, f_zb,
     e_px, e_big, e_ya, e_yb, squares, sq_kappa,
     rows_x, gather_map, spread_map,
@@ -188,9 +182,7 @@
 
     arrivals = []
     for i, (source, target) in enumerate((
-        (diff_any, diff_ref), (kappa_any, kappa_ref), (depth_any, depth_ref),
-        (widen_any, widen_ref), (coefficient_any, coefficient_ref), (load_any, load_ref),
-        (vertical_any, vertical_ref), (across_any, across_ref),
+        (diff_any, diff_ref), (kappa_any, kappa_ref), (table_any, table_ref), (load_any, load_ref),
     )):
         copy = pltpu.make_async_copy(source, target, in_sem.at[i])
         copy.start()
@@ -243,26 +235,44 @@
 
     squares[...] = jnp.zeros_like(squares)
     sq_kappa[...] = jnp.zeros_like(sq_kappa)
-    for copy in arrivals[0:5]:
+    for copy in arrivals[0:3]:
         copy.wait()
     inside = iota((cap_y, layers), 0) < wy
+    tall = cap_x * ROWS
+    base = 4 * LANES
+    for g in range(2):
+        lanes = slice(g * LANES, (g + 1) * LANES)
+        high = table_ref[g * LANES : (g + 1) * LANES, :].astype(jnp.bfloat16)
+        low = table_ref[(g + 2) * LANES : (g + 3) * LANES, :].astype(jnp.bfloat16)
+        for k, part in enumerate((high, high, low)):
+            vertical_ref[k * LANES : (k + 1) * LANES, lanes] = part
+    high = table_ref[base : base + 2 * LANES, :].astype(jnp.bfloat16)
+    low = table_ref[base + 2 * LANES : base + 4 * LANES, :].astype(jnp.bfloat16)
+    for k, part in enumerate((high, high, low)):
+        across_ref[:, k * LANES : (k + 1) * LANES] = part
+    base = 8 * LANES
+    depth_table = jnp.concatenate(
+        [table_ref[base + k * LANES : base + (k + 1) * LANES, :] for k in range(3)], axis=1
+    )
+    base = 11 * LANES
+    widen = table_ref[base : base + 3 * tall, :]
+    base = base + 3 * tall
     for e in range(cap_x):
         keep = inside & (e < wx)
         squares[8 * e : 8 * e + cap_y, 0:layers] = jnp.where(keep, diff_ref[e], 0.0)
         sq_kappa[8 * e : 8 * e + cap_y, 0:layers] = jnp.where(keep, kappa_ref[e], 0.0)
-    deep = jnp.dot(squares[...], depth_ref[...], precision=HIGHEST, preferred_element_type=jnp.float32)
+    deep = jnp.dot(squares[...], depth_table, precision=HIGHEST, preferred_element_type=jnp.float32)
     deep_kappa = jnp.dot(
-        sq_kappa[...], depth_ref[:, 0:LANES], precision=HIGHEST, preferred_element_type=jnp.float32
-    )
-    tall = cap_x * ROWS
+        sq_kappa[...], depth_table[:, 0:LANES], precision=HIGHEST, preferred_element_type=jnp.float32
+    )
     big = jnp.dot(
-        widen_ref[0:tall, :],
+        widen[0:tall, :],
         jnp.concatenate([deep, deep_kappa], axis=1),
         precision=HIGHEST,
         preferred_element_type=jnp.float32,
     )
     both = jnp.dot(
-        widen_ref[tall : 3 * tall, :],
+        widen[tall : 3 * tall, :],
         deep[:, 0:LANES],
         precision=HIGHEST,
         preferred_element_type=jnp.float32,
@@ -286,8 +296,8 @@
     sources = (
         (f_za, e_big, 0), (f_zb, e_big, 1), (f_mass, e_big, 2), (f_ya, e_ya, 0), (f_yb, e_yb, 0),
     )
-    row_factor = coefficient_ref[0:ROWS, :]
-    depth_factor = coefficient_ref[ROWS : ROWS + 1, :]
+    row_factor = table_ref[base : base + ROWS, :]
+    depth_factor = table_ref[base + ROWS : base + ROWS + 1, :]
     corner = float(STIFF[7, 7])
 
     def fill_plane(x, e, b):
@@ -318,7 +328,7 @@
     row = iota((slots_y, LANES), 0)
     real = iota((slots_y, LANES), 1) <= 7 * layers
     f_r[...] = jnp.zeros_like(f_r)
-    arrivals[5].wait()
+    arrivals[3].wait()
 
     def take(x, _):
         value = jnp.where(x < end_x, load_ref[x], jnp.where(x == end_x, load_ref[slots_x - 1], 0.0))
@@ -413,7 +423,7 @@
                 ref[pl.ds(pl.multiple_of(i * chunk, chunk), chunk), :].reshape(4, ROWS, LANES), axis=0
             )
 
-        middle = lax.fori_loop(0, chunks, add, zero_plane)
+        middle = lax.fori_loop(0, chunks, add, zero_plane, unroll=True)
         low, high = 0.5 * has_left * ref[0:ROWS, :], 0.5 * has_right * high_plane(ref)
         sums = [jnp.zeros((8, LANES), jnp.float32)] * 3
         for dx, value in ((-1, low), (0, middle - low - high), (1, high)):
@@ -537,7 +547,7 @@
                 f_im[plane(7 * e + b), :] = results[b]
             return results[7]
 
-        carried = lax.fori_loop(0, cap_x, along_x, zero_plane)
+        carried = lax.fori_loop(0, cap_x, along_x, zero_plane, unroll=True)
         f_im[plane(7 * cap_x), :] = carried
 
         def along_rest(i, product):
@@ -561,7 +571,7 @@
             f_im[rows, :] = image
             return product + jnp.sum((value * image).reshape(chunk // 8, 8, LANES), axis=0)
 
-        product = lax.fori_loop(0, chunks, along_rest, jnp.zeros((8, LANES), jnp.float32))
+        product = lax.fori_loop(0, chunks, along_rest, jnp.zeros((8, LANES), jnp.float32), unroll=True)
         return total(product)
 
     reduce_start(0, f_r)
@@ -616,8 +626,6 @@
     jacobi = total(lax.fori_loop(0, planes, invert, zero_plane))
     for copy in ring:
         copy.wait()
-    for copy in arrivals[6:]:
-        copy.wait()
     reduce_middle(0, [])
     grid, _, through = reduce_finish(0, None)
     coarse = coarse_planes(grid)
@@ -673,7 +681,9 @@
                 f_z[here, :] = value
                 return sums[0] + share * scaled * resid, sums[1] + share * value * image
 
-            jacobi, cross = lax.fori_loop(0, planes, advance, (zero_plane, zero_plane))
+            jacobi, cross = lax.fori_loop(
+                0, planes, advance, (zero_plane, zero_plane), unroll=True
+            )
             jacobi, cross = total(jacobi), total(cross)
         else:
             last_s[...] = scalar_row([own, cross, jacobi])
@@ -722,13 +732,13 @@
     hbm = pl.BlockSpec(memory_space=pltpu.HBM)
     tall = cap_x * ROWS
     dma = pltpu.SemaphoreType.DMA
-    constants = [jnp.asarray(table) for table in tables(cap_x, cap_y, layers)]
+    table = jnp.asarray(tables(cap_x, cap_y, layers))
 
     def room(*shape, dtype=f32):
         return pltpu.VMEM(shape, dtype)
 
-    scratch = [room(*array.shape, dtype=array.dtype) for array in (right_side, diffusion, kappa)]
-    scratch += [room(*array.shape, dtype=array.dtype) for array in constants]
+    scratch = [room(*array.shape) for array in (right_side, diffusion, kappa, table)]
+    scratch += [room(3 * LANES, 2 * LANES, dtype=bf16), room(2 * LANES, 3 * LANES, dtype=bf16)]
     scratch += [room(PLANES * ROWS, LANES)] * 13
     scratch += [
         room(tall + 2 * ROWS, LANES),
@@ -759,20 +769,20 @@
         room(far, 1, LANES),
         room(1, LANES),
         room(near, 1, LANES),
-        dma((8,)), dma((1,)), dma((near,)), dma((near,)), dma((8,)), dma((8,)),
+        dma((4,)), dma((1,)), dma((near,)), dma((near,)), dma((8,)), dma((8,)),
         dma((halos, 8)), dma((halos, 8)), dma((ITERS, 3)), dma((ITERS, 3)), dma((2,)), dma((2,)),
     ]
     shape = jax.ShapeDtypeStruct(right_side.shape, f32)
     return pl.pallas_call(
         functools.partial(kernel, nx, ny, cap_x, cap_y, layers, bx, by),
         out_shape=(shape, shape),
-        in_specs=[smem, smem] + [hbm] * 9,
+        in_specs=[smem, smem] + [hbm] * 5,
         out_specs=(vmem, vmem),
         scratch_shapes=scratch,
         compiler_params=pltpu.CompilerParams(
-            collective_id=0, has_side_effects=True, vmem_limit_bytes=48 * 1024 * 1024
+            collective_id=0, has_side_effects=True, vmem_limit_bytes=60 * 1024 * 1024
         ),
-    )(widths_x, widths_y, right_side, diffusion, kappa, factor, *constants)
+    )(widths_x, widths_y, right_side, diffusion, kappa, factor, table)
 
 
 def solution(mesh):

time: 123 us -> 109 us (0.89)
  Pallas kernels: 111 us -> 104 us
  local copies, waits for them, and re-layouts: 9.73 us -> 2.93 us
    unnamed x20 -> x4, local copies, waits for them, and re-layouts: 9.73 us -> 2.93 us
    pallas_call x1, Pallas kernels: 111 us -> 104 us  [body(): pl.pallas_call(functools.partial(kernel, nx, ny, cap_x, cap_y, layers, bx...]
where the time goes in v3:
time: 109 us
  Pallas kernels  104 us (95%)
  local copies, waits for them, and re-layouts  2.93 us (3%)
  between operations  1.94 us (2%)
    pallas_call x1, Pallas kernels, body(): pl.pallas_call(functools.partial(kernel, nx, ny, cap_x, cap_y, layers, bx...  104 us
    unnamed x4, local copies, waits for them, and re-layouts  2.93 us

profile of v3, /device:TPU:1, one launch (start us, length us, event | category | flops | bytes accessed | tf_op | source)
XLA Modules:
  0.0 109.3 jit_solution(7935889431433921656)
XLA Ops:
  1.9 104.4 %shard_map.86 = (f32[43,29,128]{2,1,0:T(8,128)}, f32[43,29,128]{2,1,0:T(8,128)}) custom-call(s32[1]{0:T(128)S(6)} %copy.11.wx_ref, s32[1]{0:T(128)S(6)} %copy.12.wy_ref, f32[43,29,128]{2,1,0:T(8,128)} %load_any.1, f32[6,4,18]{2,1,0:T(4,128)} %diff_any.1, f32[6,4,18]{2,1,0:T(4,128)} %kappa_any.1, f32[16,8192]{1,0:T(8,128)} %factor_any.1, ...), custom_call_target="tpu_custom_call" | custom-call | tf_op jit(solution)/shard_map/pallas_call | solution.py:776
  106.3 0.0 copy-start
  106.4 2.1 %copy.13 = f32[43,29,128]{2,1,0:T(8,128)} copy(f32[43,29,128]{2,1,0:T(8,128)} %get-tuple-element.4) | data formatting | bytes 1276928
  108.4 0.0 copy-done
  108.4 0.9 copy.14
Async XLA Ops:
  106.3 2.1 %copy-start = (f32[43,29,128]{2,1,0:T(8,128)S(1)}, f32[43,29,128]{2,1,0:T(8,128)}, u32[]{:S(2)}) copy-start(f32[43,29,128]{2,1,0:T(8,128)} %get-tuple-element.5) | copy-start | bytes 1915396

commit v4 on v3

--- a/solution.py
+++ b/solution.py
@@ -175,8 +175,8 @@
         greet(across(lax.rem(block_id + o, far)))
         return 0
 
-    lax.fori_loop(1, near, greet_near, 0)
-    lax.fori_loop(1, far, greet_far, 0)
+    lax.fori_loop(1, near, greet_near, 0, unroll=True)
+    lax.fori_loop(1, far, greet_far, 0, unroll=True)
     for dx, dy in DIRECTIONS:
         greet(beside(dx, dy))
 
@@ -215,8 +215,6 @@
     has_left, has_right = flag(p > 0), flag(p < nx - 1)
     has_below, has_above = flag(q > 0), flag(q < ny - 1)
 
-    pl.semaphore_wait(barrier, near + far - 2 + len(DIRECTIONS))
-
     def scatter_copy(o):
         peer = lax.rem(mine + o, near)
         return remote(
@@ -231,7 +229,100 @@
         scatter_copy(o).start()
         return 0
 
-    lax.fori_loop(1, near, scatter, 0)
+    zero_plane = jnp.zeros((ROWS, LANES), jnp.float32)
+    slots_x, slots_y = load_ref.shape[0], load_ref.shape[1]
+    row = iota((slots_y, LANES), 0)
+    real = iota((slots_y, LANES), 1) <= 7 * layers
+    f_r[...] = jnp.zeros_like(f_r)
+    arrivals[3].wait()
+
+    def take(x, _):
+        value = jnp.where(x < end_x, load_ref[x], jnp.where(x == end_x, load_ref[slots_x - 1], 0.0))
+        last = value[slots_y - 1 : slots_y, :]
+        value = jnp.where(row < end_y, value, jnp.where(row == end_y, last, 0.0))
+        f_r[pl.ds(pl.multiple_of(x * ROWS, ROWS), slots_y), :] = jnp.where(real, value, 0.0)
+        return 0
+
+    lax.fori_loop(0, slots_x, take, 0)
+
+    def high_plane(ref):
+        value = jnp.zeros((ROWS, LANES), jnp.float32)
+        for j in range(1, cap_x + 1):
+            value = value + jnp.where(wx == j, ref[7 * j * ROWS : (7 * j + 1) * ROWS, :], 0.0)
+        return value
+
+    def side(j):
+        return pl.ds(7 * j, PLANES, stride=ROWS)
+
+    def high_row(plane_value):
+        value = jnp.zeros((1, LANES), jnp.float32)
+        for j in range(1, cap_y + 1):
+            value = value + jnp.where(wy == j, plane_value[7 * j : 7 * j + 1, :], 0.0)
+        return value
+
+    def halo_copies(h):
+        copies = []
+        for k, (dx, dy) in enumerate(DIRECTIONS):
+            if dy == 0:
+                slot = (h, 0 if dx > 0 else 1)
+                source, target = halo_sx.at[slot], halo_rx.at[slot]
+            elif dx == 0:
+                slot = (h, 0 if dy > 0 else 1)
+                source, target = halo_sy.at[slot], halo_ry.at[slot]
+            else:
+                source, target = halo_sc.at[h, k - 4], halo_rc.at[h, k - 4]
+            copies.append(remote(source, target, h_send.at[h, k], h_recv.at[h, k], beside(dx, dy)))
+        return copies
+
+    def halo_pack(h, ref):
+        low, high = ref[0:ROWS, :], high_plane(ref)
+        halo_sx[h, 0] = high
+        halo_sx[h, 1] = low
+        above = jnp.zeros((PLANES, LANES), jnp.float32)
+        for j in range(1, cap_y + 1):
+            above = above + jnp.where(wy == j, ref[side(j), :], 0.0)
+        halo_sy[h, 0] = above
+        halo_sy[h, 1] = ref[side(0), :]
+        rows = (high_row(high), high[0:1, :], high_row(low), low[0:1, :])
+        for k, value in enumerate(rows):
+            halo_sc[h, k] = jnp.broadcast_to(value, (8, LANES))
+
+    def halo_send(h):
+        copies = halo_copies(h)
+        for copy in copies:
+            copy.start()
+        return copies
+
+    def halo_start(h, ref):
+        halo_pack(h, ref)
+        return halo_send(h)
+
+    place = iota((PLANES, LANES), 0)
+
+    def halo_finish(h, ref, copies):
+        for copy in copies:
+            copy.wait()
+        ref[0:ROWS, :] = ref[0:ROWS, :] + has_left * halo_rx[h, 0]
+        from_right = has_right * halo_rx[h, 1]
+        for j in range(1, cap_x + 1):
+            rows = slice(7 * j * ROWS, (7 * j + 1) * ROWS)
+            ref[rows, :] = ref[rows, :] + jnp.where(wx == j, from_right, 0.0)
+
+        def line(side_value, first, second):
+            side_value = side_value + jnp.where(place == 0, has_left * first[0:1, :], 0.0)
+            return side_value + jnp.where(place == end_x, has_right * second[0:1, :], 0.0)
+
+        below = has_below * line(halo_ry[h, 0], halo_rc[h, 0], halo_rc[h, 2])
+        above = has_above * line(halo_ry[h, 1], halo_rc[h, 1], halo_rc[h, 3])
+        ref[side(0), :] = ref[side(0), :] + below
+        for j in range(1, cap_y + 1):
+            ref[side(j), :] = ref[side(j), :] + jnp.where(wy == j, above, 0.0)
+
+    halo_pack(0, f_r)
+    pl.semaphore_wait(barrier, near + far - 2 + len(DIRECTIONS))
+
+    load_copies = halo_send(0)
+    lax.fori_loop(1, near, scatter, 0, unroll=True)
 
     squares[...] = jnp.zeros_like(squares)
     sq_kappa[...] = jnp.zeros_like(sq_kappa)
@@ -277,18 +368,17 @@
         precision=HIGHEST,
         preferred_element_type=jnp.float32,
     )
-    zero_plane = jnp.zeros((ROWS, LANES), jnp.float32)
     for ref in (e_px, e_ya, e_yb):
         ref[0:ROWS, :] = zero_plane
         ref[tall + ROWS : tall + 2 * ROWS, :] = zero_plane
-    for place in (0, tall + ROWS):
-        e_big[place : place + ROWS, :] = jnp.zeros((ROWS, 3 * LANES), jnp.float32)
+    for edge in (0, tall + ROWS):
+        e_big[edge : edge + ROWS, :] = jnp.zeros((ROWS, 3 * LANES), jnp.float32)
     e_px[ROWS : ROWS + tall, :] = big[:, 0:LANES]
     e_big[ROWS : ROWS + tall, :] = big[:, LANES : 4 * LANES]
     e_ya[ROWS : ROWS + tall, :] = both[0:tall]
     e_yb[ROWS : ROWS + tall, :] = both[tall : 2 * tall]
 
-    fields = (f_z, f_im, f_r, f_inv, f_mass, f_ya, f_yb, f_za, f_zb)
+    fields = (f_z, f_im, f_inv, f_mass, f_ya, f_yb, f_za, f_zb)
     for ref in fields:
         for x in range(7 * cap_x, PLANES):
             ref[x * ROWS : (x + 1) * ROWS, :] = zero_plane
@@ -324,88 +414,6 @@
     lax.fori_loop(0, cap_x, fill, 0)
     fill_plane(7 * cap_x, cap_x, 0)
 
-    slots_x, slots_y = load_ref.shape[0], load_ref.shape[1]
-    row = iota((slots_y, LANES), 0)
-    real = iota((slots_y, LANES), 1) <= 7 * layers
-    f_r[...] = jnp.zeros_like(f_r)
-    arrivals[3].wait()
-
-    def take(x, _):
-        value = jnp.where(x < end_x, load_ref[x], jnp.where(x == end_x, load_ref[slots_x - 1], 0.0))
-        last = value[slots_y - 1 : slots_y, :]
-        value = jnp.where(row < end_y, value, jnp.where(row == end_y, last, 0.0))
-        f_r[pl.ds(pl.multiple_of(x * ROWS, ROWS), slots_y), :] = jnp.where(real, value, 0.0)
-        return 0
-
-    lax.fori_loop(0, slots_x, take, 0)
-
-    def high_plane(ref):
-        value = jnp.zeros((ROWS, LANES), jnp.float32)
-        for j in range(1, cap_x + 1):
-            value = value + jnp.where(wx == j, ref[7 * j * ROWS : (7 * j + 1) * ROWS, :], 0.0)
-        return value
-
-    def side(j):
-        return pl.ds(7 * j, PLANES, stride=ROWS)
-
-    def high_row(plane_value):
-        value = jnp.zeros((1, LANES), jnp.float32)
-        for j in range(1, cap_y + 1):
-            value = value + jnp.where(wy == j, plane_value[7 * j : 7 * j + 1, :], 0.0)
-        return value
-
-    def halo_copies(h):
-        copies = []
-        for k, (dx, dy) in enumerate(DIRECTIONS):
-            if dy == 0:
-                slot = (h, 0 if dx > 0 else 1)
-                source, target = halo_sx.at[slot], halo_rx.at[slot]
-            elif dx == 0:
-                slot = (h, 0 if dy > 0 else 1)
-                source, target = halo_sy.at[slot], halo_ry.at[slot]
-            else:
-                source, target = halo_sc.at[h, k - 4], halo_rc.at[h, k - 4]
-            copies.append(remote(source, target, h_send.at[h, k], h_recv.at[h, k], beside(dx, dy)))
-        return copies
-
-    def halo_start(h, ref):
-        low, high = ref[0:ROWS, :], high_plane(ref)
-        halo_sx[h, 0] = high
-        halo_sx[h, 1] = low
-        above = jnp.zeros((PLANES, LANES), jnp.float32)
-        for j in range(1, cap_y + 1):
-            above = above + jnp.where(wy == j, ref[side(j), :], 0.0)
-        halo_sy[h, 0] = above
-        halo_sy[h, 1] = ref[side(0), :]
-        rows = (high_row(high), high[0:1, :], high_row(low), low[0:1, :])
-        for k, value in enumerate(rows):
-            halo_sc[h, k] = jnp.broadcast_to(value, (8, LANES))
-        copies = halo_copies(h)
-        for copy in copies:
-            copy.start()
-        return copies
-
-    place = iota((PLANES, LANES), 0)
-
-    def halo_finish(h, ref, copies):
-        for copy in copies:
-            copy.wait()
-        ref[0:ROWS, :] = ref[0:ROWS, :] + has_left * halo_rx[h, 0]
-        from_right = has_right * halo_rx[h, 1]
-        for j in range(1, cap_x + 1):
-            rows = slice(7 * j * ROWS, (7 * j + 1) * ROWS)
-            ref[rows, :] = ref[rows, :] + jnp.where(wx == j, from_right, 0.0)
-
-        def line(side_value, first, second):
-            side_value = side_value + jnp.where(place == 0, has_left * first[0:1, :], 0.0)
-            return side_value + jnp.where(place == end_x, has_right * second[0:1, :], 0.0)
-
-        below = has_below * line(halo_ry[h, 0], halo_rc[h, 0], halo_rc[h, 2])
-        above = has_above * line(halo_ry[h, 1], halo_rc[h, 1], halo_rc[h, 3])
-        ref[side(0), :] = ref[side(0), :] + below
-        for j in range(1, cap_y + 1):
-            ref[side(j), :] = ref[side(j), :] + jnp.where(wy == j, above, 0.0)
-
     deep_node, deep_lane = iota((LANES, LANES), 0), iota((LANES, LANES), 1)
     for dy in (-1, 0, 1):
         part = slice((dy + 1) * LANES, (dy + 2) * LANES)
@@ -417,7 +425,7 @@
     chunk = 4 * ROWS
     chunks = (7 * cap_x + 4) // 4
 
-    def coarse_sums(ref):
+    def coarse_sums(ref, assembled):
         def add(i, value):
             return value + jnp.sum(
                 ref[pl.ds(pl.multiple_of(i * chunk, chunk), chunk), :].reshape(4, ROWS, LANES), axis=0
@@ -426,11 +434,12 @@
         middle = lax.fori_loop(0, chunks, add, zero_plane, unroll=True)
         low, high = 0.5 * has_left * ref[0:ROWS, :], 0.5 * has_right * high_plane(ref)
         sums = [jnp.zeros((8, LANES), jnp.float32)] * 3
-        for dx, value in ((-1, low), (0, middle - low - high), (1, high)):
+        middle = middle - low - high
+        for dx, value in ((0, middle),) if assembled else ((-1, low), (0, middle), (1, high)):
             below = 0.5 * has_below * value[0:1, :]
             above = 0.5 * has_above * high_row(value)
             centre = jnp.sum(value, axis=0, keepdims=True) - below - above
-            for k, profile in enumerate((below, centre, above)):
+            for k, profile in ((1, centre),) if assembled else enumerate((below, centre, above)):
                 sums[k] = sums[k] + jnp.where(grid_row == bi + 1 + dx, profile, 0.0)
         return exact_dot(jnp.concatenate(sums, axis=1), gather_map[...])
 
@@ -447,11 +456,11 @@
             remote(source, target.at[me], send, recv, device(lax.rem(me + o, count))).start()
             return 0
 
-        lax.fori_loop(1, count, go, 0)
+        lax.fori_loop(1, count, go, 0, unroll=True)
         target[me] = source[...]
 
-    def reduce_start(a, ref):
-        grid_s[a] = coarse_sums(ref)
+    def reduce_start(a, ref, assembled=False):
+        grid_s[a] = coarse_sums(ref, assembled)
         exchange_start(
             grid_s.at[a], grid_r.at[a], near, mine, in_block, r_send.at[a, 0], r_recv.at[a, 0]
         )
@@ -469,13 +478,15 @@
 
     grid_rows, grid_lanes = bx + 2, (by + 2) * 16
 
-    def reduce_middle(a, scalars):
+    def reduce_middle(a, scalars, inner=False):
         wait_in(grid_r.at[a], near - 1, r_send.at[a, 0], r_recv.at[a, 0])
         turned = jnp.sum(grid_r[a], axis=0).T
         value = jnp.zeros((8, width), jnp.float32)
-        for i in range(grid_rows):
-            product = rows_x[i] * turned[0:grid_lanes, i : i + 1]
-            value = value + jnp.sum(product.reshape(grid_lanes // 8, 8, width), axis=0)
+        rim = 1 if inner else 0
+        part = slice(16 * rim, grid_lanes - 16 * rim)
+        for i in range(rim, grid_rows - rim):
+            product = rows_x[i, part, :] * turned[part, i : i + 1]
+            value = value + jnp.sum(product.reshape(-1, 8, width), axis=0)
         value = jnp.sum(value, axis=0, keepdims=True)
         for g in range(groups):
             chunk_s[a, g : g + 1, :] = value[:, g * LANES : (g + 1) * LANES]
@@ -574,9 +585,9 @@
         product = lax.fori_loop(0, chunks, along_rest, jnp.zeros((8, LANES), jnp.float32), unroll=True)
         return total(product)
 
-    reduce_start(0, f_r)
-    load_copies = halo_start(0, f_r)
     diagonal_copies = halo_start(1, f_inv)
+    halo_finish(0, f_r, load_copies)
+    reduce_start(0, f_r, True)
 
     own_rows.wait()
 
@@ -598,10 +609,8 @@
             ring_recv.at[k],
             beside(dx * bx, dy * by),
         )
-        copy.start()
         ring.append(copy)
 
-    halo_finish(0, f_r, load_copies)
     halo_finish(1, f_inv, diagonal_copies)
     share_low = jnp.where(row32 == 0, 1.0 - 0.5 * has_below, 1.0)
     share_row = jnp.where(row32 == end_y, 1.0 - 0.5 * has_above, share_low)
@@ -624,9 +633,13 @@
 
     planes = 7 * cap_x + 1
     jacobi = total(lax.fori_loop(0, planes, invert, zero_plane))
+    for copy in ring[2:4]:
+        copy.start()
+    reduce_middle(0, [], True)
+    for copy in ring[0:2] + ring[4:]:
+        copy.start()
     for copy in ring:
         copy.wait()
-    reduce_middle(0, [])
     grid, _, through = reduce_finish(0, None)
     coarse = coarse_planes(grid)
 
@@ -772,7 +785,7 @@
         dma((4,)), dma((1,)), dma((near,)), dma((near,)), dma((8,)), dma((8,)),
         dma((halos, 8)), dma((halos, 8)), dma((ITERS, 3)), dma((ITERS, 3)), dma((2,)), dma((2,)),
     ]
-    shape = jax.ShapeDtypeStruct(right_side.shape, f32)
+    shape = pltpu.VMEM(right_side.shape, f32)
     return pl.pallas_call(
         functools.partial(kernel, nx, ny, cap_x, cap_y, layers, bx, by),
         out_shape=(shape, shape),
@@ -780,7 +793,7 @@
         out_specs=(vmem, vmem),
         scratch_shapes=scratch,
         compiler_params=pltpu.CompilerParams(
-            collective_id=0, has_side_effects=True, vmem_limit_bytes=60 * 1024 * 1024
+            collective_id=0, has_side_effects=True, vmem_limit_bytes=56 * 1024 * 1024
         ),
     )(widths_x, widths_y, right_side, diffusion, kappa, factor, table)
 

time: 109 us -> 101 us (0.927)
  Pallas kernels: 104 us -> 97.5 us
  local copies, waits for them, and re-layouts: 2.93 us -> 1.71 us
    pallas_call x1, Pallas kernels: 104 us -> 97.5 us  [body(): pl.pallas_call(functools.partial(kernel, nx, ny, cap_x, cap_y, layers, bx...]
    unnamed x4 -> x2, local copies, waits for them, and re-layouts: 2.93 us -> 1.71 us
where the time goes in v4:
time: 101 us
  Pallas kernels  97.5 us (97%)
  between operations  1.93 us (2%)
  local copies, waits for them, and re-layouts  1.71 us (2%)
    pallas_call x1, Pallas kernels, body(): pl.pallas_call(functools.partial(kernel, nx, ny, cap_x, cap_y, layers, bx...  97.5 us

profile of v4, /device:TPU:1, one launch (start us, length us, event | category | flops | bytes accessed | tf_op | source)
XLA Modules:
  0.0 101.2 jit_solution(18284127505555189050)
XLA Ops:
  1.9 97.5 %shard_map.86 = (f32[43,29,128]{2,1,0:T(8,128)S(1)}, f32[43,29,128]{2,1,0:T(8,128)S(1)}) custom-call(s32[1]{0:T(128)S(6)} %copy.13.wx_ref, s32[1]{0:T(128)S(6)} %copy.14.wy_ref, f32[43,29,128]{2,1,0:T(8,128)} %load_any.1, f32[6,4,18]{2,1,0:T(4,128)} %diff_any.1, f32[6,4,18]{2,1,0:T(4,128)} %kappa_any.1, f32[16,8192]{1,0:T(8,128)} %factor_any.1, ...), custom_call_target="tpu_custom_call" | custom-call | tf_op jit(solution)/shard_map/pallas_call | solution.py:789
  99.5 0.9 copy.11
  100.3 0.9 copy.12

commit v5 on v4

--- a/solution.py
+++ b/solution.py
@@ -139,9 +139,9 @@
     e_px, e_big, e_ya, e_yb, squares, sq_kappa,
     rows_x, gather_map, spread_map,
     halo_sx, halo_sy, halo_sc, halo_rx, halo_ry, halo_rc,
-    grid_s, grid_r, chunk_s, chunk_r, back_s, back_r, last_s, last_r, end_s, end_r,
+    grid_s, grid_r, chunk_s, chunk_r, back_s, back_r, last_s, last_r, end_s, end_r, line_s, line_r,
     in_sem, own_sem, x_send, x_recv, ring_send, ring_recv,
-    h_send, h_recv, r_send, r_recv, l_send, l_recv,
+    h_send, h_recv, r_send, r_recv, l_send, l_recv, line_send, line_recv,
 ):
     p, q = lax.axis_index("gx"), lax.axis_index("gy")
     wx, wy = wx_ref[0], wy_ref[0]
@@ -495,13 +495,14 @@
             chunk_s.at[a], chunk_r.at[a], far, block_id, across, r_send.at[a, 1], r_recv.at[a, 1]
         )
 
-    def reduce_finish(a, extra):
+    def reduce_finish(a, extra, inner=False):
         wait_in(chunk_r.at[a], far - 1, r_send.at[a, 1], r_recv.at[a, 1])
         sums = jnp.sum(chunk_r[a], axis=0)
         through = sums[0:groups, :]
         turned = jnp.zeros((grid_lanes, LANES), jnp.float32)
         wide_lane = iota((grid_lanes, LANES), 1)
-        for i in range(grid_rows):
+        rim = 1 if inner else 0
+        for i in range(rim, grid_rows - rim):
             product = rows_x[i, :, 0:LANES] * through[0:1, :]
             for g in range(1, groups):
                 product = product + rows_x[i, :, g * LANES : (g + 1) * LANES] * through[g : g + 1, :]
@@ -638,9 +639,19 @@
     reduce_middle(0, [], True)
     for copy in ring[0:2] + ring[4:]:
         copy.start()
-    for copy in ring:
+    for copy in ring[2:4]:
         copy.wait()
-    grid, _, through = reduce_finish(0, None)
+    grid, _, through = reduce_finish(0, None, True)
+    line_s[...] = jnp.sum(jnp.where(grid_row == bi + 1, grid, 0.0), axis=0, keepdims=True)
+    lines = [
+        remote(line_s, line_r.at[k], line_send.at[k], line_recv.at[k], beside(dx, 0))
+        for k, dx in enumerate((1, -1))
+    ]
+    for copy in lines:
+        copy.start()
+    for copy in lines:
+        copy.wait()
+    grid = jnp.where(grid_row == bi, line_r[0], jnp.where(grid_row == bi + 2, line_r[1], grid))
     coarse = coarse_planes(grid)
 
     def begin(x, _):
@@ -649,7 +660,7 @@
         f_z[plane(x), :] = inverse * f_r[plane(x), :] + value
         return 0
 
-    lax.fori_loop(0, planes, begin, 0)
+    lax.fori_loop(0, planes, begin, 0, unroll=True)
 
     cross = jnp.zeros((1, 1), jnp.float32)
     beta, rho, curvature = cross, None, cross
@@ -667,6 +678,9 @@
         if i + 1 < ITERS:
             reduce_start(i + 1, f_im)
             image_copies = halo_start(2 + i, f_im)
+            if i == 0:
+                for copy in ring[0:2] + ring[4:]:
+                    copy.wait()
             reduce_middle(i + 1, [own, cross, jacobi])
             halo_finish(2 + i, f_im, image_copies)
             grid_q, values, through_q = reduce_finish(i + 1, squared)
@@ -729,7 +743,7 @@
         put(residual_ref, x, jnp.where(x < end_x, resid, 0.0))
         return 0
 
-    lax.fori_loop(0, planes, finish, 0)
+    lax.fori_loop(0, planes, finish, 0, unroll=True)
     put(solution_ref, slots_x - 1, high_plane(f_sol))
     put(residual_ref, slots_x - 1, high_plane(f_r))
 
@@ -782,8 +796,11 @@
         room(far, 1, LANES),
         room(1, LANES),
         room(near, 1, LANES),
+        room(1, LANES),
+        room(2, 1, LANES),
         dma((4,)), dma((1,)), dma((near,)), dma((near,)), dma((8,)), dma((8,)),
         dma((halos, 8)), dma((halos, 8)), dma((ITERS, 3)), dma((ITERS, 3)), dma((2,)), dma((2,)),
+        dma((2,)), dma((2,)),
     ]
     shape = pltpu.VMEM(right_side.shape, f32)
     return pl.pallas_call(

time: 101 us -> 98.9 us (0.979)
  Pallas kernels: 97.5 us -> 95.1 us
    pallas_call x1, Pallas kernels: 97.5 us -> 95.1 us  [body(): pl.pallas_call(functools.partial(kernel, nx, ny, cap_x, cap_y, layers, bx...]
where the time goes in v5:
time: 98.9 us; the launch traced here: 98.8 us
  Pallas kernels  95.1 us (96%)
  between operations  1.93 us (2%)
  local copies, waits for them, and re-layouts  1.71 us (2%)
    pallas_call x1, Pallas kernels, body(): pl.pallas_call(functools.partial(kernel, nx, ny, cap_x, cap_y, layers, bx...  95.1 us

profile of v5, /device:TPU:1, one launch (start us, length us, event | category | flops | bytes accessed | tf_op | source)
XLA Modules:
  0.0 98.8 jit_solution(15531273666464008712)
XLA Ops:
  1.9 95.1 %shard_map.86 = (f32[43,29,128]{2,1,0:T(8,128)S(1)}, f32[43,29,128]{2,1,0:T(8,128)S(1)}) custom-call(s32[1]{0:T(128)S(6)} %copy.13.wx_ref, s32[1]{0:T(128)S(6)} %copy.14.wy_ref, f32[43,29,128]{2,1,0:T(8,128)} %load_any.1, f32[6,4,18]{2,1,0:T(4,128)} %diff_any.1, f32[6,4,18]{2,1,0:T(4,128)} %kappa_any.1, f32[16,8192]{1,0:T(8,128)} %factor_any.1, ...), custom_call_target="tpu_custom_call" | custom-call | tf_op jit(solution)/shard_map/pallas_call | solution.py:806
  97.0 0.9 copy.11
  97.9 0.9 copy.12
